TPU v7x, 128 devices: a whole 4x4x4 slice. The times are simulated.
128 devices in a mesh: space: 32 (over z, y, core), orb: 4 (over x).
Axes of the slice: x: 4, y: 4, z: 4, core: 2. Of those that a mesh axis runs over, the one named last changes fastest.
Arguments:
- orbitals: float32 [8, 32768, 256], P('orb', 'space'), may hold values from -6 to 6
- near_source: int32 [32768, 27], P('space'), may hold values from 0 to 32767, as said below
- far_leaf: int32 [32768, 108], P('space'), may hold values from 0 to 32767, as said below
- far_mid: int32 [4096, 108], P('space'), may hold values from 0 to 4095, as said below
- far_top: int32 [512, 108], P('space'), may hold values from 0 to 511, as said below
- leaf_basis: bfloat16 [64, 256], replicated, may hold values from -0.375 to 0.375
- near_table: bfloat16 [27, 256, 256], replicated, may hold values from -0.078125 to 0.078125
- transfer: bfloat16 [8, 64, 64], replicated, may hold values from -0.75 to 0.75
- coupling: bfloat16 [108, 64, 64], replicated, may hold values from -0.078125 to 0.078125
- pair_transfer: bfloat16 [2, 64, 64], replicated, may hold values from -0.75 to 0.75
- coarse_coupling: bfloat16 [4, 64, 64], replicated, may hold values from -0.4375 to 0.4375
Outputs:
- relaxed: float32 [8, 32768, 256], P('orb', 'space')
Inputs may be any that keep to these rules, and one draw needn't show every extreme that they name: `near_source`: with layer(t) = t // 64: every entry of leaf t lies in a layer at most 1 from layer(t); entry 13 is t itself; entry 0 is the leaf at t's transverse position one layer away. `far_leaf`: with layer(t) = t // 64: every entry of box t lies in a layer 2 or 3 away from layer(t); entry 0 is exactly 3 layers away. `far_mid`: with layer(t) = t // 16: every entry of box t lies in a layer 2 or 3 away from layer(t); entry 0 is exactly 3 layers away. `far_top`: with layer(t) = t // 4: every entry of box t lies in a layer 2 or 3 away from layer(t); entry 0 is exactly 3 layers away.
All inputs are finite; a program needn't handle non-finite values.
Results may differ from a plain program's by a relative error of at most 0.012.
Values may be sent and summed in bfloat16 or wider, within the bound.
A program may use at most 192 MiB of HBM per device.

v0:
```python
import jax
import jax.numpy as jnp
from jax import lax
from jax.sharding import PartitionSpec as P

SIDE = 8


relax_step = 0.1


def padded(cells, sides, width):
    for axis, dim in sides:
        count = lax.axis_size(axis)
        ends = count - 1
        head = lax.slice_in_dim(cells, 0, width, axis=dim)
        tail = lax.slice_in_dim(cells, cells.shape[dim] - width, cells.shape[dim], axis=dim)
        cells = jnp.concatenate(
            [
                lax.ppermute(tail, axis, [(i, (i + 1) % count) for i in range(ends)]),
                cells,
                lax.ppermute(head, axis, [((i + 1) % count, i) for i in range(ends)]),
            ],
            axis=dim,
        )
    return cells


def leaf_project(density, leaf_basis):
    return jnp.einsum(
        "olp,rp->lor", density, leaf_basis, preferred_element_type=jnp.float32
    ).astype(jnp.bfloat16)


def octant_up(moments, side_boxes, transfer):
    node_count, orbits, rank_width = moments.shape
    layers = node_count // (side_boxes * side_boxes)
    half_side = side_boxes // 2
    shaped = moments.reshape(layers // 2, 2, half_side, 2, half_side, 2, orbits, rank_width)
    octant_grid = transfer.reshape(2, 2, 2, rank_width, rank_width)
    parents = jnp.einsum(
        "apbqcuos,pqusr->abcor", shaped, octant_grid, preferred_element_type=jnp.float32
    )
    return parents.reshape(-1, orbits, rank_width).astype(jnp.bfloat16)


def octant_down(coeffs, side_boxes, transfer):
    node_count, orbits, rank_width = coeffs.shape
    layers = node_count // (side_boxes * side_boxes)
    shaped = coeffs.reshape(layers, side_boxes, side_boxes, orbits, rank_width)
    octant_grid = transfer.reshape(2, 2, 2, rank_width, rank_width)
    children = jnp.einsum(
        "abcor,pqusr->apbqcuos", shaped, octant_grid, preferred_element_type=jnp.float32
    )
    return children.reshape(-1, orbits, rank_width)


def couple_rows(moments, sources, coupling, scale):
    node_count, orbits, rank_width = moments.shape
    flattened = moments.reshape(node_count, orbits * rank_width)
    identity = jnp.eye(orbits, dtype=coupling.dtype)
    running = None
    for column_start in range(0, sources.shape[1], 27):
        block_coupling = coupling[column_start : column_start + 27]
        widened = jnp.einsum("ab,krs->kasbr", identity, block_coupling).reshape(
            block_coupling.shape[0], orbits * rank_width, orbits * rank_width
        )
        picked = jnp.take(flattened, sources[:, column_start : column_start + 27], axis=0)
        piece_sum = jnp.einsum("lkx,kxy->ly", picked, widened, preferred_element_type=jnp.float32)
        running = piece_sum if running is None else running + piece_sum
    return scale * running.reshape(-1, orbits, rank_width)


def near_sum(density, sources, near_table):
    running = None
    for column_start in range(0, sources.shape[1], 9):
        picked = jnp.take(density, sources[:, column_start : column_start + 9], axis=1)
        piece_sum = jnp.einsum(
            "olkq,kpq->olp",
            picked,
            near_table[column_start : column_start + 9],
            preferred_element_type=jnp.float32,
        )
        running = piece_sum if running is None else running + piece_sum
    return running


def shifted(values, offset):
    node_count = values.shape[0]
    if abs(offset) >= node_count:
        return jnp.zeros_like(values)
    empty = jnp.zeros((abs(offset), values.shape[1], values.shape[2]), values.dtype)
    if offset > 0:
        return jnp.concatenate([values[offset:], empty], axis=0)
    return jnp.concatenate([empty, values[:offset]], axis=0)


def coarse_couple(moments, coarse_coupling, scale):
    node_count = moments.shape[0]
    odd_rows = (jnp.arange(node_count) % 2).astype(jnp.float32)[:, None, None]
    even_rows = 1.0 - odd_rows

    def apply_matrix(which, offset):
        return jnp.einsum(
            "nos,rs->nor",
            shifted(moments, offset),
            coarse_coupling[which],
            preferred_element_type=jnp.float32,
        )

    running = (
        apply_matrix(1, -2)
        + apply_matrix(2, 2)
        + even_rows * apply_matrix(3, 3)
        + odd_rows * apply_matrix(0, -3)
    )
    return scale * running


def coarse_up(moments, pair_transfer):
    node_count, orbits, rank_width = moments.shape
    shaped = moments.reshape(-1, 2, orbits, rank_width)
    return jnp.einsum(
        "apos,psr->aor", shaped, pair_transfer, preferred_element_type=jnp.float32
    ).astype(jnp.bfloat16)


def coarse_down(coeffs, pair_transfer):
    children = jnp.einsum(
        "aor,psr->apos", coeffs, pair_transfer, preferred_element_type=jnp.float32
    )
    return children.reshape(-1, coeffs.shape[1], coeffs.shape[2])


def coarse_tree(cube_moments, coarse_coupling, pair_transfer):
    levels = [cube_moments]
    while levels[-1].shape[0] > 1:
        levels.append(coarse_up(levels[-1], pair_transfer))
    top_level = len(levels) - 1
    coeffs = coarse_couple(levels[top_level], coarse_coupling, 0.5 ** (3 + top_level)).astype(
        jnp.bfloat16
    )
    for depth_level in range(top_level - 1, -1, -1):
        pushed = coarse_down(coeffs, pair_transfer)
        coupled = coarse_couple(levels[depth_level], coarse_coupling, 0.5 ** (3 + depth_level))
        coeffs = (coupled + pushed).astype(jnp.bfloat16)
    return coeffs


def shards(
    orbitals,
    near_source,
    far_leaf,
    far_mid,
    far_top,
    leaf_basis,
    near_table,
    transfer,
    coupling,
    pair_transfer,
    coarse_coupling,
):
    orbits, leaf_count, points = orbitals.shape
    rank_size = leaf_basis.shape[0]
    device = lax.axis_index("space")
    density = (orbitals * orbitals).astype(jnp.bfloat16)
    layer_size = SIDE * SIDE
    reach_leaves = 12 * layer_size
    density_ext = padded(density, (("space", 1),), layer_size)
    near_start = device * leaf_count - layer_size
    local_moments = leaf_project(density, leaf_basis)
    flattened = local_moments.reshape(leaf_count, orbits * rank_size)
    leaf_ext = padded(flattened, (("space", 0),), reach_leaves).reshape(-1, orbits, rank_size)
    near_field = near_sum(density_ext, near_source - near_start, near_table)
    mid_ext = octant_up(leaf_ext, SIDE, transfer)
    top_ext = octant_up(mid_ext, SIDE // 2, transfer)
    top_count = leaf_count // 64
    mid_count = leaf_count // 8
    top_rim = reach_leaves // 64
    mid_rim = reach_leaves // 8
    top_local = top_ext[top_rim : top_rim + top_count]
    cube_local = octant_up(top_local, SIDE // 4, transfer)
    cube_rows = cube_local.shape[0]
    cube_all = lax.all_gather(
        cube_local.reshape(cube_rows, orbits * rank_size), "space", axis=0, tiled=True
    ).reshape(-1, orbits, rank_size)
    cube_coeffs = coarse_tree(cube_all, coarse_coupling, pair_transfer)
    cube_own = lax.dynamic_slice_in_dim(cube_coeffs, device * cube_rows, cube_rows, 0)
    top_coeffs = (
        couple_rows(top_ext, far_top - (device * top_count - top_rim), coupling, 0.25)
        + octant_down(cube_own, SIDE // 8, transfer)
    ).astype(jnp.bfloat16)
    mid_coeffs = (
        couple_rows(mid_ext, far_mid - (device * mid_count - mid_rim), coupling, 0.5)
        + octant_down(top_coeffs, SIDE // 4, transfer)
    ).astype(jnp.bfloat16)
    leaf_coeffs = (
        couple_rows(leaf_ext, far_leaf - (device * leaf_count - reach_leaves), coupling, 1.0)
        + octant_down(mid_coeffs, SIDE // 2, transfer)
    ).astype(jnp.bfloat16)
    far_field = jnp.einsum(
        "lor,rp->olp", leaf_coeffs, leaf_basis, preferred_element_type=jnp.float32
    )
    potential = near_field + far_field
    hartree = lax.psum(jnp.sum(potential, axis=0).astype(jnp.bfloat16), "orb").astype(jnp.float32)
    return orbitals - relax_step * (hartree[None] - potential) * orbitals


def solution(mesh):
    placed = (
        P("orb", "space", None),
        P("space", None),
        P("space", None),
        P("space", None),
        P("space", None),
        P(),
        P(),
        P(),
        P(),
        P(),
        P(),
    )
    return jax.shard_map(
        shards, mesh=mesh, in_specs=placed, out_specs=P("orb", "space", None), check_vma=False
    )
```

profile of v0, /device:TPU:0, one launch (start us, length us, event | category | flops | bytes accessed | tf_op | source)
XLA Modules:
  0.0 1078.0 jit_solution(17902328975907240493)
XLA Ops:
  55.0 9.0 multiply_bitcast_fusion
  105.5 7.3 copy.392
  112.7 71.8 %gather_fusion.2 = bf16[9216,2,256]{2,1,0:T(2,128)(2,1)} fusion(bf16[2,1152,256]{2,0,1:T(2,128)(2,1)S(1)} %copy.392, s32[9216]{0:T(1024)S(1)} %broadcast_clamp_fusion.4), kind=kCustom, calls=%fused_computation.5.clone | custom fusion | bytes 18911232 | tf_op jit(solution)/shard_map/jit(_take)/gather | solution.py:77
  184.6 71.8 %gather_fusion.1 = bf16[9216,2,256]{2,1,0:T(2,128)(2,1)} fusion(bf16[2,1152,256]{2,0,1:T(2,128)(2,1)S(1)} %copy.392, s32[9216]{0:T(1024)S(1)} %broadcast_clamp_fusion.5), kind=kCustom, calls=%fused_computation.4.clone | custom fusion | bytes 18911232 | tf_op jit(solution)/shard_map/jit(_take)/gather | solution.py:77
  256.4 71.8 %gather_fusion = bf16[9216,2,256]{2,1,0:T(2,128)(2,1)} fusion(bf16[2,1152,256]{2,0,1:T(2,128)(2,1)S(1)} %copy.392, s32[9216]{0:T(1024)S(1)} %broadcast_clamp_fusion.6), kind=kCustom, calls=%fused_computation.clone | custom fusion | bytes 18911232 | tf_op jit(solution)/shard_map/jit(_take)/gather | solution.py:77
  328.2 18.5 %fusion.2 = bf16[2,1024,9,256]{3,0,2,1:T(2,128)(2,1)S(1)} fusion(bf16[1024,9,2,256]{3,2,1,0:T(2,128)(2,1)} %bitcast.386, pred[1024,9]{1,0:T(8,128)(4,1)S(1)} %copy-done.18), kind=kLoop, calls=%fused_computation.20 | loop fusion | flops 4718592 | bytes 18883584 | tf_op jit(solution)/shard_map/jit(_take)/select_n | solution.py:77
  350.8 16.6 %fusion.1 = bf16[2,1024,9,256]{3,0,2,1:T(2,128)(2,1)S(1)} fusion(bf16[1024,9,2,256]{3,2,1,0:T(2,128)(2,1)S(1)} %bitcast.385, pred[1024,9]{1,0:T(8,128)(4,1)S(1)} %copy-done.19), kind=kLoop, calls=%fused_computation.19 | loop fusion | flops 4718592 | bytes 18883584 | tf_op jit(solution)/shard_map/jit(_take)/select_n | solution.py:77
  367.5 18.0 %fusion = bf16[2,1024,9,256]{3,0,2,1:T(2,128)(2,1)} fusion(bf16[1024,9,2,256]{3,2,1,0:T(2,128)(2,1)S(1)} %bitcast.382, pred[1024,9]{1,0:T(8,128)(4,1)S(1)} %copy-done.20), kind=kLoop, calls=%fused_computation.18 | loop fusion | flops 4718592 | bytes 18883584 | tf_op jit(solution)/shard_map/jit(_take)/select_n | solution.py:77
  395.5 28.1 %all-gather = bf16[32,2,128]{2,1,0:T(2,128)(2,1)S(1)} all-gather(bf16[1,2,128]{2,1,0:T(2,128)(2,1)S(1)} %reshape.425), channel_id=1, replica_groups=mesh['space'=32,'orb'=4] {'space'}, dimensions={0}, use_global_device_ids=true | all-gather | bytes 16896 | tf_op jit(solution)/shard_map/all_gather | solution.py:184
  449.5 8.2 gather_fusion.10
  475.8 7.1 gather_fusion.8
  504.7 96.4 %gather_fusion.3 = bf16[27648,128]{1,0:T(8,128)(2,1)} fusion(bf16[2560,128]{1,0:T(8,128)(2,1)S(1)} %pad_maximum_fusion.1, s32[27648]{0:T(1024)S(1)} %broadcast_clamp_fusion.3), kind=kCustom, calls=%fused_computation.1.clone | custom fusion | bytes 14266368 | tf_op jit(solution)/shard_map/jit(_take)/gather | solution.py:68
  601.1 11.9 %reshape.448 = bf16[1024,27,128]{2,1,0:T(8,128)(2,1)} reshape(bf16[27648,128]{1,0:T(8,128)(2,1)} %gather_fusion.3) | data formatting | bytes 14155776 | tf_op jit(solution)/shard_map/jit(_take)/gather | solution.py:68
  613.1 15.5 %broadcast_select_fusion.6 = bf16[1024,27,128]{2,1,0:T(8,128)(2,1)S(1)} fusion(bf16[1024,27,128]{2,1,0:T(8,128)(2,1)} %reshape.448, pred[1024,27]{1,0:T(8,128)(4,1)S(1)} %copy-done.17), kind=kLoop, calls=%fused_computation.30 | loop fusion | flops 3538944 | bytes 14183424 | tf_op jit(solution)/shard_map/jit(_take)/select_n | solution.py:68
  632.9 96.4 %gather_fusion.4 = bf16[27648,128]{1,0:T(8,128)(2,1)} fusion(bf16[2560,128]{1,0:T(8,128)(2,1)S(1)} %pad_maximum_fusion.1, s32[27648]{0:T(1024)S(1)} %broadcast_clamp_fusion.2), kind=kCustom, calls=%fused_computation.6.clone | custom fusion | bytes 14266368 | tf_op jit(solution)/shard_map/jit(_take)/gather | solution.py:68
  729.3 11.9 %reshape.452 = bf16[1024,27,128]{2,1,0:T(8,128)(2,1)} reshape(bf16[27648,128]{1,0:T(8,128)(2,1)} %gather_fusion.4) | data formatting | bytes 14155776 | tf_op jit(solution)/shard_map/jit(_take)/gather | solution.py:68
  741.2 96.4 %gather_fusion.5 = bf16[27648,128]{1,0:T(8,128)(2,1)} fusion(bf16[2560,128]{1,0:T(8,128)(2,1)S(1)} %pad_maximum_fusion.1, s32[27648]{0:T(1024)S(1)} %broadcast_clamp_fusion.1), kind=kCustom, calls=%fused_computation.7.clone | custom fusion | bytes 14266368 | tf_op jit(solution)/shard_map/jit(_take)/gather | solution.py:68
  837.6 11.9 %reshape.456 = bf16[1024,27,128]{2,1,0:T(8,128)(2,1)} reshape(bf16[27648,128]{1,0:T(8,128)(2,1)} %gather_fusion.5) | data formatting | bytes 14155776 | tf_op jit(solution)/shard_map/jit(_take)/gather | solution.py:68
  849.5 96.4 %gather_fusion.6 = bf16[27648,128]{1,0:T(8,128)(2,1)} fusion(bf16[2560,128]{1,0:T(8,128)(2,1)S(1)} %pad_maximum_fusion.1, s32[27648]{0:T(1024)S(1)} %copy-done.4), kind=kCustom, calls=%fused_computation.8.clone | custom fusion | bytes 14266368 | tf_op jit(solution)/shard_map/jit(_take)/gather | solution.py:68
  945.9 11.9 %reshape.460 = bf16[1024,27,128]{2,1,0:T(8,128)(2,1)} reshape(bf16[27648,128]{1,0:T(8,128)(2,1)} %gather_fusion.6) | data formatting | bytes 14155776 | tf_op jit(solution)/shard_map/jit(_take)/gather | solution.py:68
  957.9 15.4 %broadcast_select_fusion.5 = bf16[1024,27,128]{2,1,0:T(8,128)(2,1)S(1)} fusion(bf16[1024,27,128]{2,1,0:T(8,128)(2,1)} %reshape.452, pred[1024,27]{1,0:T(8,128)(4,1)S(1)} %copy-done.14), kind=kLoop, calls=%fused_computation.29 | loop fusion | flops 3538944 | bytes 14183424 | tf_op jit(solution)/shard_map/jit(_take)/select_n | solution.py:68
  977.7 15.7 %broadcast_select_fusion.4 = bf16[1024,27,128]{2,1,0:T(8,128)(2,1)S(1)} fusion(bf16[1024,27,128]{2,1,0:T(8,128)(2,1)} %reshape.456, pred[1024,27]{1,0:T(8,128)(4,1)S(1)} %copy-done.15), kind=kLoop, calls=%fused_computation.28 | loop fusion | flops 3538944 | bytes 14183424 | tf_op jit(solution)/shard_map/jit(_take)/select_n | solution.py:68
  997.8 13.7 %broadcast_select_fusion.3 = bf16[1024,27,128]{2,1,0:T(8,128)(2,1)S(1)} fusion(bf16[1024,27,128]{2,1,0:T(8,128)(2,1)S(1)} %bitcast.388, pred[1024,27]{1,0:T(8,128)(4,1)S(1)} %copy-done.16), kind=kLoop, calls=%fused_computation.27 | loop fusion | flops 3538944 | bytes 14183424 | tf_op jit(solution)/shard_map/jit(_take)/select_n | solution.py:68
  1023.5 43.0 %all-reduce.22.cloned.1.call-done = bf16[1024,256]{1,0:T(8,128)(2,1)} async-done(((bf16[1024,256]{1,0:T(8,128)(2,1)}), bf16[1024,256]{1,0:T(8,128)(2,1)}) %all-reduce.22.cloned.1.call-update) | async-done | bytes 524304 | tf_op jit(solution)/shard_map/psum | solution.py:205
  (343 shorter events, 197.9 us)
Async XLA Ops:
  6.5 387.6 %copy-start = (bf16[8,64,64]{2,1,0:T(8,128)(2,1)S(1)}, bf16[8,64,64]{2,1,0:T(8,128)(2,1)}, u32[]{:S(2)}) copy-start(bf16[8,64,64]{2,1,0:T(8,128)(2,1)} %param.26) | copy-start | bytes 196612
  6.5 29.9 %copy-start.11 = (bf16[4,64,64]{2,1,0:T(8,128)(2,1)S(1)}, bf16[4,64,64]{2,1,0:T(8,128)(2,1)}, u32[]{:S(2)}) copy-start(bf16[4,64,64]{2,1,0:T(8,128)(2,1)} %param.29) | copy-start | bytes 98308
  6.5 25.2 %copy-start.24 = (s32[1024,108]{0,1:T(8,128)S(1)}, s32[1024,108]{0,1:T(8,128)}, u32[]{:S(2)}) copy-start(s32[1024,108]{0,1:T(8,128)} %param.21) | copy-start | bytes 1327108
  6.5 30.7 %copy-start.9 = (bf16[2,64,64]{2,1,0:T(8,128)(2,1)S(1)}, bf16[2,64,64]{2,1,0:T(8,128)(2,1)}, u32[]{:S(2)}) copy-start(bf16[2,64,64]{2,1,0:T(8,128)(2,1)} %param.28) | copy-start | bytes 49156
  6.5 34.3 %copy-start.2 = (bf16[108,64,64]{0,2,1:T(8,128)(2,1)S(1)}, bf16[108,64,64]{0,2,1:T(8,128)(2,1)}, u32[]{:S(2)}) copy-start(bf16[108,64,64]{0,2,1:T(8,128)(2,1)} %param.27) | copy-start | bytes 2654212
  6.5 1059.9 %all-reduce.22.cloned.1.call-start = ((), (), s32[]{:S(2)}) async-start(), calls=%async_computation | async-start | bytes 1048576 | tf_op jit(solution)/shard_map/psum | solution.py:205
  10.5 379.0 %collective-permute-start.2 = (bf16[768,128]{1,0:T(8,128)(2,1)}, bf16[768,128]{1,0:T(8,128)(2,1)}, u32[]{:S(2)}, u32[]{:S(2)}) collective-permute-start(bf16[768,128]{1,0:T(8,128)(2,1)} %copy.403), channel_id=1, source_target_pairs={{0,4},{4,8},{8,12},{12,16},{16,20},{20,24},{24,28},{28,32},{32,36}... | collective-permute-start | bytes 589832 | tf_op jit(solution)/shard_map/ppermute | solution.py:20
  13.3 376.3 %collective-permute-start.3 = (bf16[768,128]{1,0:T(8,128)(2,1)}, bf16[768,128]{1,0:T(8,128)(2,1)}, u32[]{:S(2)}, u32[]{:S(2)}) collective-permute-start(bf16[768,128]{1,0:T(8,128)(2,1)} %copy.404), channel_id=1, source_target_pairs={{4,0},{8,4},{12,8},{16,12},{20,16},{24,20},{28,24},{32,28},{36,32}... | collective-permute-start | bytes 589832 | tf_op jit(solution)/shard_map/ppermute | solution.py:22
  15.3 89.3 %collective-permute-start = (bf16[2,64,256]{2,1,0:T(8,128)(2,1)}, bf16[2,64,256]{2,1,0:T(8,128)(2,1)}, u32[]{:S(2)}, u32[]{:S(2)}) collective-permute-start(bf16[2,64,256]{2,1,0:T(8,128)(2,1)} %get-tuple-element.6), channel_id=1, source_target_pairs={{0,4},{4,8},{8,12},{12,16},{16,20},{20,24},{24,28},{28,32},{32,36}... | collective-permute-start | bytes 196616 | tf_op jit(solution)/shard_map/ppermute | solution.py:20
  20.1 84.4 %collective-permute-start.1 = (bf16[2,64,256]{2,1,0:T(8,128)(2,1)}, bf16[2,64,256]{2,1,0:T(8,128)(2,1)}, u32[]{:S(2)}, u32[]{:S(2)}) collective-permute-start(bf16[2,64,256]{2,1,0:T(8,128)(2,1)} %get-tuple-element.8), channel_id=1, source_target_pairs={{4,0},{8,4},{12,8},{16,12},{20,16},{24,20},{28,24},{32,28},{36,32}... | collective-permute-start | bytes 196616 | tf_op jit(solution)/shard_map/ppermute | solution.py:22
  64.0 25.9 %copy-start.23 = (s32[1024,27]{0,1:T(8,128)S(1)}, s32[1024,27]{0,1:T(8,128)}, u32[]{:S(2)}) copy-start(s32[1024,27]{0,1:T(8,128)} %get-tuple-element.21) | copy-start | bytes 331780
  64.0 27.3 %copy-start.22 = (s32[1024,27]{0,1:T(8,128)S(1)}, s32[1024,27]{0,1:T(8,128)}, u32[]{:S(2)}) copy-start(s32[1024,27]{0,1:T(8,128)} %get-tuple-element.20) | copy-start | bytes 331780
  67.5 26.1 %copy-start.21 = (s32[1024,27]{0,1:T(8,128)S(1)}, s32[1024,27]{0,1:T(8,128)}, u32[]{:S(2)}) copy-start(s32[1024,27]{0,1:T(8,128)} %get-tuple-element.19) | copy-start | bytes 331780
  73.2 26.3 %copy-start.29 = (s32[1024,9]{0,1:T(8,128)S(1)}, s32[1024,9]{0,1:T(8,128)}, u32[]{:S(2)}) copy-start(s32[1024,9]{0,1:T(8,128)} %get-tuple-element.30) | copy-start | bytes 110596
  256.4 71.8 %copy-start.18 = (pred[1024,9]{1,0:T(8,128)(4,1)S(1)}, pred[1024,9]{1,0:T(8,128)(4,1)}, u32[]{:S(2)}) copy-start(pred[1024,9]{1,0:T(8,128)(4,1)} %copy.398) | copy-start | bytes 27652
  389.5 34.2 %copy-start.10 = (bf16[2,64,64]{2,1,0:T(8,128)(2,1)S(1)}, bf16[2,64,64]{2,1,0:T(8,128)(2,1)}, u32[]{:S(2)}) copy-start(bf16[2,64,64]{2,1,0:T(8,128)(2,1)} %param.28) | copy-start | bytes 49156
  389.5 35.2 %copy-start.12 = (bf16[4,64,64]{2,1,0:T(8,128)(2,1)S(1)}, bf16[4,64,64]{2,1,0:T(8,128)(2,1)}, u32[]{:S(2)}) copy-start(bf16[4,64,64]{2,1,0:T(8,128)(2,1)} %param.29) | copy-start | bytes 98308
  389.5 47.4 %copy-start.37 = (s32[1024]{0:T(1024)S(1)}, s32[1024]{0:T(1024)}, u32[]{:S(2)}) copy-start(s32[1024]{0:T(1024)} %pad_clamp_fusion.7) | copy-start | bytes 12292
  389.5 49.0 %copy-start.38 = (s32[1024]{0:T(1024)S(1)}, s32[1024]{0:T(1024)}, u32[]{:S(2)}) copy-start(s32[1024]{0:T(1024)} %pad_clamp_fusion.6) | copy-start | bytes 12292
  389.5 51.2 %copy-start.39 = (s32[1024]{0:T(1024)S(1)}, s32[1024]{0:T(1024)}, u32[]{:S(2)}) copy-start(s32[1024]{0:T(1024)} %pad_clamp_fusion.5) | copy-start | bytes 12292
  394.7 54.3 %copy-start.6 = (bf16[27,128,128]{2,1,0:T(8,128)(2,1)S(1)}, bf16[27,128,128]{2,1,0:T(8,128)(2,1)}, u32[]{:S(2)}) copy-start(bf16[27,128,128]{2,1,0:T(8,128)(2,1)} %reshape.258) | copy-start | bytes 2654212
  973.3 24.5 %slice-start.6 = ((s8[8388608]{0:T(1024)(128)(4,1)}), s8[4194304]{0:T(1024)(128)(4,1)S(1)}, s32[]{:S(2)}) async-start(s8[8388608]{0:T(1024)(128)(4,1)} %bitcast.387), calls=%async_computation.7 | async-start | bytes 8388608
  1016.5 51.1 %copy-start.3 = (f32[2,1024,256]{2,1,0:T(8,128)S(1)}, f32[2,1024,256]{2,1,0:T(8,128)}, u32[]{:S(2)}) copy-start(f32[2,1024,256]{2,1,0:T(8,128)} %param.19) | copy-start | bytes 6291460
  1016.5 54.3 %copy-start.1 = (bf16[8,64,64]{2,1,0:T(8,128)(2,1)S(1)}, bf16[8,64,64]{2,1,0:T(8,128)(2,1)}, u32[]{:S(2)}) copy-start(bf16[8,64,64]{2,1,0:T(8,128)(2,1)} %param.26) | copy-start | bytes 196612
  (39 other events, 542.9 us)
Sparse Core Ops, SparseCore 0:
  1023.6 42.8 all-reduce.21
where the time goes:
time: 1090 us; the launch traced here: 1080 us
  local copies, waits for them, and re-layouts  761 us (70%)
  other arithmetic  162 us (15%)
  matrix products  58.8 us (5%)
  waiting for transfers between devices  43 us (4%)
  blocking collectives  28.1 us (3%)
  between operations  15 us (1%)
    gather x24, local copies, waits for them, and re-layouts, couple_rows(): jnp.take(flattened, sources[:, column_start:column_start + 27], axis=0)  475 us
    gather x3, local copies, waits for them, and re-layouts, near_sum(): jnp.take(density, sources[:, column_start:column_start + 9], axis=1)  215 us
    select_n x13, other arithmetic, couple_rows(): jnp.take(flattened, sources[:, column_start:column_start + 27], axis=0)  74.5 us
    select_n x4, other arithmetic, near_sum(): jnp.take(density, sources[:, column_start:column_start + 9], axis=1)  53.8 us
    psum x1, waiting for transfers between devices, shards(): lax.psum(jnp.sum(potential, axis=0).astype(jnp.bfloat16), 'orb')  43 us
    all_gather x1, blocking collectives, shards(): lax.all_gather(cube_local.reshape(cube_rows, orbits * rank_size), 'space'...  28.1 us
    dot_general x12, matrix products, couple_rows(): jnp.einsum('lkx,kxy->ly', picked, widened, preferred_element_type=jnp.flo...  26 us
  transfers between devices with their start and end apart: 5, of which 1 were waited for; matrix products, arithmetic and copies ran while one was open for 34% of the time, Pallas kernels for 0%

commit v1 on v0

v1 whole, which is shorter than its diff:
```python
import jax
import jax.numpy as jnp
from jax import lax
from jax.experimental import pallas as pl
from jax.experimental.pallas import tpu as pltpu
from jax.sharding import PartitionSpec as P

BF = jnp.bfloat16
F32 = jnp.float32
NN = (((1,), (0,)), ((), ()))
NT = (((1,), (1,)), ((), ()))
RELAX_STEP = 0.1
PARAMS = pltpu.CompilerParams(vmem_limit_bytes=56 << 20)


def dot(a, b, dims=NN):
    return lax.dot_general(a, b, dims, preferred_element_type=F32)


def iota(shape, dim):
    return lax.broadcasted_iota(jnp.int32, shape, dim)


def ones_where(mask):
    return jnp.where(mask, 1.0, 0.0).astype(BF)


def one_hot(column, rows, width):
    return ones_where(iota((rows, width), 1) == column)


def twice(matrices):
    zero = jnp.zeros_like(matrices)
    top = jnp.concatenate([matrices, zero], axis=-1)
    low = jnp.concatenate([zero, matrices], axis=-1)
    return jnp.concatenate([top, low], axis=-2)


def octant_picker(parents, half, width):
    row, col = iota((8 * parents, width), 0), iota((8 * parents, width), 1)
    octant, b = row // parents, row % parents
    z, y, x = b // (half * half), (b // half) % half, b % half
    dz, dy, dx = octant // 4, (octant // 2) % 2, octant % 2
    side = 2 * half
    child = ((2 * z + dz) * side + 2 * y + dy) * side + 2 * x + dx
    return ones_where(child == col)


def merge_up(picked, parents, transfer_ref):
    total = None
    for octant in range(8):
        part = dot(picked[octant * parents : (octant + 1) * parents], transfer_ref[octant])
        total = part if total is None else total + part
    return total.astype(BF)


def moments_kernel(
    orb_ref, basis_ref, transfer_ref, dens_ref, leaf_ref, mid_ref, top_ref, cube_ref, head_ref, tail_ref
):
    step = pl.program_id(0)
    for o in range(2):
        values = orb_ref[o]
        dens_ref[:, o * 256 : (o + 1) * 256] = (values * values).astype(BF)
    leaf = dot(dens_ref[...], basis_ref[...], NT).astype(BF)
    leaf_ref[...] = leaf
    picked = dot(octant_picker(32, 4, 256), leaf).astype(BF)
    mid = merge_up(picked, 32, transfer_ref)
    mid_ref[pl.ds(pl.multiple_of(step * 32, 32), 32), :] = mid

    @pl.when(step == 0)
    def _():
        head_ref[0:192, :] = leaf[0:192]

    @pl.when(step == 3)
    def _():
        tail_ref[0:192, :] = leaf[64:256]
        mids = mid_ref[...]
        top = merge_up(dot(octant_picker(16, 2, 128), mids).astype(BF), 16, transfer_ref)
        top_ref[...] = top
        cube_ref[...] = merge_up(dot(octant_picker(16, 1, 16), top).astype(BF), 16, transfer_ref)
        head_ref[192:240, :] = mids[0:48]
        tail_ref[192:240, :] = mids[80:128]
        head_ref[240:256, :] = top
        tail_ref[240:256, :] = top


def moments(orbitals, basis2, transfer2):
    whole = lambda *shape: pl.BlockSpec(shape, lambda c: (0,) * len(shape))
    shape = lambda *s: jax.ShapeDtypeStruct(s, BF)
    return pl.pallas_call(
        moments_kernel,
        grid=(4,),
        in_specs=[pl.BlockSpec((2, 256, 256), lambda c: (0, c, 0)), whole(128, 512), whole(8, 128, 128)],
        out_specs=[
            pl.BlockSpec((256, 512), lambda c: (c, 0)),
            pl.BlockSpec((256, 128), lambda c: (c, 0)),
            whole(128, 128),
            whole(16, 128),
            whole(16, 128),
            whole(256, 128),
            whole(256, 128),
        ],
        out_shape=[
            shape(1024, 512),
            shape(1024, 128),
            shape(128, 128),
            shape(16, 128),
            shape(16, 128),
            shape(256, 128),
            shape(256, 128),
        ],
        compiler_params=PARAMS,
        cost_estimate=pl.CostEstimate(flops=400_000_000, bytes_accessed=4 << 20, transcendentals=0),
        name="moments",
    )(orbitals, basis2, transfer2)


def near_kernel(
    source_ref, prev_ref, dens_ref, next_ref, table_ref, near_ref, sum_ref, ext_ref, hot_ref, pick_ref
):
    step = pl.program_id(0)

    @pl.when(step == 0)
    def _():
        ext_ref[0:64, :] = prev_ref[...]
        ext_ref[64:1088, :] = dens_ref[...]
        ext_ref[1088:1152, :] = next_ref[...]

    for part in range(2):
        place = (source_ref[part * 128 : (part + 1) * 128, :] + (64 + 128 * part)) & 255
        for k in range(27):
            hot_ref[k * 128 : (k + 1) * 128, :] = one_hot(place[:, k : k + 1], 128, 256)
        base = pl.multiple_of(step * 256 + part * 128, 128)
        for o in range(2):
            rows = ext_ref[pl.ds(base, 256), o * 256 : (o + 1) * 256]
            at = o * 256 + part * 128
            for first in range(0, 27, 9):
                picked = dot(hot_ref[first * 128 : (first + 9) * 128, :], rows).astype(BF)
                for k in range(9):
                    pick_ref[at : at + 128, (first + k) * 256 : (first + k + 1) * 256] = picked[
                        k * 128 : (k + 1) * 128
                    ]
    total = None
    for k in range(27):
        part = dot(pick_ref[:, k * 256 : (k + 1) * 256], table_ref[k], NT)
        total = part if total is None else total + part
    near_ref[:, :256] = total[:256]
    near_ref[:, 256:] = total[256:]
    sum_ref[...] = (total[:256] + total[256:]).astype(BF)


def near_field(sources, prev, density, after, table):
    whole = lambda *shape: pl.BlockSpec(shape, lambda c: (0,) * len(shape))
    rows = lambda *shape: pl.BlockSpec(shape, lambda c: (c, 0))
    return pl.pallas_call(
        near_kernel,
        grid=(4,),
        in_specs=[rows(256, 27), whole(64, 512), whole(1024, 512), whole(64, 512), whole(27, 256, 256)],
        out_specs=[rows(256, 512), rows(256, 256)],
        out_shape=[jax.ShapeDtypeStruct((1024, 512), F32), jax.ShapeDtypeStruct((1024, 256), BF)],
        scratch_shapes=[
            pltpu.VMEM((1152, 512), BF),
            pltpu.VMEM((27 * 128, 256), BF),
            pltpu.VMEM((512, 27 * 256), BF),
        ],
        compiler_params=PARAMS,
        cost_estimate=pl.CostEstimate(flops=15_000_000_000, bytes_accessed=8 << 20, transcendentals=0),
        name="near",
    )(sources, prev, density, after, table)


def far_kernel(
    leaf_list, mid_list, top_list, prev_ref, leaf_ref, mid_ref, top_ref, next_ref, coupling_ref,
    out_ref, ext_ref, midx_ref, topx_ref, weight_ref, hot_ref, pick_ref,
):
    step = pl.program_id(0)
    device = lax.axis_index("space")

    @pl.when(step == 0)
    def _():
        ext_ref[0:192, :] = prev_ref[0:192]
        ext_ref[192:1216, :] = leaf_ref[...]
        ext_ref[1216:1408, :] = next_ref[0:192]
        midx_ref[0:48, :] = prev_ref[192:240]
        midx_ref[48:176, :] = mid_ref[...]
        midx_ref[176:224, :] = next_ref[192:240]
        midx_ref[224:256, :] = jnp.zeros((32, 128), BF)
        topx_ref[0:16, :] = prev_ref[240:256]
        topx_ref[16:32, :] = top_ref[...]
        topx_ref[32:48, :] = next_ref[240:256]
        topx_ref[48:128, :] = jnp.zeros((80, 128), BF)
        zero = jnp.zeros((64, 64), BF)
        for k in range(108):
            matrix = coupling_ref[k]
            weight_ref[0:64, k * 128 : (k + 1) * 128] = jnp.concatenate([matrix, zero], axis=1)
            weight_ref[64:128, k * 128 : (k + 1) * 128] = jnp.concatenate([zero, matrix], axis=1)

    def pick(place, rows, at, table):
        width = table.shape[0]
        for k in range(108):
            hot_ref[k * rows : (k + 1) * rows, :width] = one_hot(place[:, k : k + 1], rows, width)
        for first in range(0, 108, 12):
            picked = dot(hot_ref[first * rows : (first + 12) * rows, :width], table).astype(BF)
            for k in range(12):
                pick_ref[at : at + rows, (first + k) * 128 : (first + k + 1) * 128] = picked[
                    k * rows : (k + 1) * rows
                ]

    @pl.when(step < 4)
    def _():
        for part in range(4):
            base = pl.multiple_of(step * 256 + part * 64, 64)
            offset = (leaf_list[part * 64 : (part + 1) * 64, :] - base + 192) & 1023
            place = jnp.where(offset < 128, offset, offset - 192)
            table = jnp.concatenate([ext_ref[pl.ds(base, 128), :], ext_ref[pl.ds(base + 320, 128), :]], axis=0)
            pick(place, 64, part * 64, table)

    @pl.when(step == 4)
    def _():
        for part in range(2):
            place = mid_list[part * 64 : (part + 1) * 64, :] - (device * 128 - 48)
            pick(place, 64, part * 64, midx_ref[...])
        pick(top_list[...] - (device * 16 - 16), 16, 128, topx_ref[...])

    out_ref[...] = dot(pick_ref[...], weight_ref[...], NT)


def far_sums(far_leaf, far_mid, far_top, prev, leaf, mid, top, after, coupling):
    whole = lambda *shape: pl.BlockSpec(shape, lambda c: (0,) * len(shape))
    return pl.pallas_call(
        far_kernel,
        grid=(5,),
        in_specs=[
            pl.BlockSpec((256, 108), lambda c: (jnp.minimum(c, 3), 0)),
            whole(128, 108),
            whole(16, 108),
            whole(256, 128),
            whole(1024, 128),
            whole(128, 128),
            whole(16, 128),
            whole(256, 128),
            whole(108, 64, 64),
        ],
        out_specs=pl.BlockSpec((256, 128), lambda c: (c, 0)),
        out_shape=jax.ShapeDtypeStruct((1280, 128), F32),
        scratch_shapes=[
            pltpu.VMEM((1408, 128), BF),
            pltpu.VMEM((256, 128), BF),
            pltpu.VMEM((128, 128), BF),
            pltpu.VMEM((128, 108 * 128), BF),
            pltpu.VMEM((108 * 64, 256), BF),
            pltpu.VMEM((256, 108 * 128), BF),
        ],
        compiler_params=PARAMS,
        cost_estimate=pl.CostEstimate(flops=20_000_000_000, bytes_accessed=4 << 20, transcendentals=0),
        name="far",
    )(far_leaf, far_mid, far_top, prev, leaf, mid, top, after, coupling)


def tree_kernel(cube_ref, pair_ref, coarse_ref, transfer_ref, far_ref, coeff_ref, sum_ref):
    device = lax.axis_index("space")
    row, col = iota((64, 64), 0), iota((64, 64), 1)
    child = [ones_where(col == 2 * row + p) for p in range(2)]
    mother = [ones_where((col == row // 2) & (row % 2 == p)) for p in range(2)]
    shift = [
        ones_where((col == row - 3) & (row % 2 == 1)),
        ones_where(col == row - 2),
        ones_where(col == row + 2),
        ones_where((col == row + 3) & (row % 2 == 0)),
    ]
    levels = [cube_ref[...]]
    for _ in range(6):
        total = None
        for p in range(2):
            part = dot(dot(child[p], levels[-1]).astype(BF), pair_ref[p])
            total = part if total is None else total + part
        levels.append(total.astype(BF))
    coeffs = None
    for depth in range(6, -1, -1):
        total = None
        for w in range(4):
            part = dot(dot(shift[w], levels[depth]).astype(BF), coarse_ref[w], NT)
            total = part if total is None else total + part
        total = total * (0.5 ** (3 + depth))
        if coeffs is not None:
            for p in range(2):
                total = total + dot(dot(mother[p], coeffs).astype(BF), pair_ref[p], NT)
        coeffs = total.astype(BF)

    def split_down(coeffs, parents, children, half, first):
        row, col = iota((children, parents), 0), iota((children, parents), 1)
        side = 2 * half
        z, y, x = row // (side * side), (row // side) % side, row % side
        parent = ((z // 2) * half + y // 2) * half + x // 2 + first
        pulled = dot(ones_where(col == parent), coeffs).astype(BF)
        r = iota((children, 128), 0)
        octant = 4 * ((r // (side * side)) % 2) + 2 * ((r // side) % 2) + r % 2
        total = None
        for o in range(8):
            part = dot(jnp.where(octant == o, pulled, jnp.zeros_like(pulled)), transfer_ref[o], NT)
            total = part if total is None else total + part
        return total

    top = 0.25 * far_ref[1152:1168] + split_down(coeffs, 64, 16, 1, 2 * device)
    mid = 0.5 * far_ref[1024:1152] + split_down(top.astype(BF), 16, 128, 2, 0)
    leaf = far_ref[0:1024] + split_down(mid.astype(BF), 128, 1024, 4, 0)
    leaf = leaf.astype(BF)
    coeff_ref[...] = leaf
    wide = leaf.astype(F32)
    sum_ref[...] = (wide[:, :64] + wide[:, 64:]).astype(BF)


def tree_down(cubes, pair2, coarse2, transfer2, far):
    return pl.pallas_call(
        tree_kernel,
        out_shape=[jax.ShapeDtypeStruct((1024, 128), BF), jax.ShapeDtypeStruct((1024, 64), BF)],
        compiler_params=PARAMS,
        cost_estimate=pl.CostEstimate(flops=600_000_000, bytes_accessed=2 << 20, transcendentals=0),
        name="tree",
    )(cubes, pair2, coarse2, transfer2, far)


def relax_kernel(orb_ref, near_ref, coeff_ref, near_sum_ref, coeff_sum_ref, basis2_ref, basis_ref, out_ref):
    potential = near_ref[...] + dot(coeff_ref[...], basis2_ref[...])
    hartree = near_sum_ref[...].astype(F32) + dot(coeff_sum_ref[...], basis_ref[...])
    for o in range(2):
        values = orb_ref[o]
        out_ref[o] = values - RELAX_STEP * (hartree - potential[:, o * 256 : (o + 1) * 256]) * values


def relax(orbitals, near, coeffs, near_sum, coeff_sum, basis2, basis):
    whole = lambda *shape: pl.BlockSpec(shape, lambda c: (0,) * len(shape))
    rows = lambda *shape: pl.BlockSpec(shape, lambda c: (c, 0))
    block = pl.BlockSpec((2, 256, 256), lambda c: (0, c, 0))
    return pl.pallas_call(
        relax_kernel,
        grid=(4,),
        in_specs=[block, rows(256, 512), rows(256, 128), rows(256, 256), rows(256, 64), whole(128, 512), whole(64, 256)],
        out_specs=block,
        out_shape=jax.ShapeDtypeStruct((2, 1024, 256), F32),
        compiler_params=PARAMS,
        cost_estimate=pl.CostEstimate(flops=300_000_000, bytes_accessed=8 << 20, transcendentals=0),
        name="relax",
    )(orbitals, near, coeffs, near_sum, coeff_sum, basis2, basis)


def shards(
    orbitals, near_source, far_leaf, far_mid, far_top, leaf_basis, near_table, transfer, coupling, pair_transfer,
    coarse_coupling,
):
    count = lax.axis_size("space")
    to_next = [(i, i + 1) for i in range(count - 1)]
    to_prev = [(i + 1, i) for i in range(count - 1)]
    basis2 = twice(leaf_basis)
    small = twice(jnp.concatenate([transfer, pair_transfer, coarse_coupling], axis=0))
    transfer2, pair2, coarse2 = small[0:8], small[8:10], small[10:14]
    density, leaf, mid, top, cube, head, tail = moments(orbitals, basis2, transfer2)
    dens_prev = lax.ppermute(density[960:1024], "space", to_next)
    dens_next = lax.ppermute(density[0:64], "space", to_prev)
    far_prev = lax.ppermute(tail, "space", to_next)
    far_next = lax.ppermute(head, "space", to_prev)
    cubes = lax.all_gather(cube[0:2], "space", axis=0, tiled=True)
    near, near_part = near_field(near_source, dens_prev, density, dens_next, near_table)
    near_sum = lax.psum(near_part, "orb")
    far = far_sums(far_leaf, far_mid, far_top, far_prev, leaf, mid, top, far_next, coupling)
    coeffs, coeff_part = tree_down(cubes, pair2, coarse2, transfer2, far)
    near_sum, coeff_part = lax.optimization_barrier((near_sum, coeff_part))
    coeff_sum = lax.psum(coeff_part, "orb")
    return relax(orbitals, near, coeffs, near_sum, coeff_sum, basis2, leaf_basis)


def solution(mesh):
    placed = (P("orb", "space", None),) + (P("space", None),) * 4 + (P(),) * 6
    return jax.shard_map(
        shards, mesh=mesh, in_specs=placed, out_specs=P("orb", "space", None), check_vma=False
    )
```

time: 1090 us -> 198 us (0.18); the launches traced: 1080 us -> 197 us
  local copies, waits for them, and re-layouts: 761 us -> 14.3 us
  other arithmetic: 162 us -> 1.66 us
  Pallas kernels: 0 us -> 83.6 us
  matrix products: 58.8 us -> 0 us
    gather x27 -> x0, local copies, waits for them, and re-layouts: 690 us -> none  [the longest x24 475 us: couple_rows(): jnp.take(flattened, sources[:, column_start:column_start + 27], axis=0)]
    select_n x17 -> x0, other arithmetic: 128 us -> none  [the longest x13 74.5 us: couple_rows(): jnp.take(flattened, sources[:, column_start:column_start + 27], axis=0)]
    pallas_call x0 -> x5, Pallas kernels: none -> 83.6 us  [the longest x1 34.6 us: far_sums(): pl.pallas_call(far_kernel, grid=(5,), in_specs=[pl.BlockSpec((256, 108),...]
    dot_general x56 -> x0, matrix products: 58.8 us -> none  [the longest x12 26 us: couple_rows(): jnp.einsum('lkx,kxy->ly', picked, widened, preferred_element_type=jnp.flo...]
    reshape x8 -> x0, local copies, waits for them, and re-layouts: 19 us -> none  [the longest x4 16.4 us: couple_rows(): jnp.einsum('ab,krs->kasbr', identity, block_coupling)]
    slice x28 -> x4, local copies, waits for them, and re-layouts: 17 us -> 2.91 us  [the longest x3 2.03 us: shards(): transfer2, pair2, coarse2 = (small[0:8], small[8:10], small[10:14])]
    and x11 -> x0, local copies, waits for them, and re-layouts: 12.7 us -> none  [the longest x8 7.88 us: couple_rows(): jnp.take(flattened, sources[:, column_start:column_start + 27], axis=0)]
    psum x1 -> x2, waiting for transfers between devices: 43 us -> 44.7 us  [the longest x1 44.7 us: shards(): coeff_sum = lax.psum(coeff_part, 'orb')]
  transfers between devices with their start and end apart: 5 -> 6, of which waited for: 1 -> 1; matrix products, arithmetic and copies ran while one was open for 34% -> 5% of each run, Pallas kernels for 0% -> 37%
where the time goes in v1:
time: 198 us; the launch traced here: 197 us
  Pallas kernels  83.6 us (42%)
  waiting for transfers between devices  44.8 us (23%)
  blocking collectives  30.3 us (15%)
  local copies, waits for them, and re-layouts  14.3 us (7%)
  between operations  13.5 us (7%)
  starting transfers between devices  8.98 us (5%)
    psum x1, waiting for transfers between devices, shards(): coeff_sum = lax.psum(coeff_part, 'orb')  44.7 us
    pallas_call x1, Pallas kernels, far_sums(): pl.pallas_call(far_kernel, grid=(5,), in_specs=[pl.BlockSpec((256, 108),...  34.6 us
    all_gather x1, blocking collectives, shards(): cubes = lax.all_gather(cube[0:2], 'space', axis=0, tiled=True)  30.3 us
    pallas_call x1, Pallas kernels, near_field(): pl.pallas_call(near_kernel, grid=(4,), in_specs=[rows(256, 27), whole(64,...  30.1 us
    unnamed x23, local copies, waits for them, and re-layouts  10.6 us
    pallas_call x1, Pallas kernels, tree_down(): pl.pallas_call(tree_kernel, out_shape=[jax.ShapeDtypeStruct((1024, 128),...  8.27 us
    pallas_call x1, Pallas kernels, moments(): pl.pallas_call(moments_kernel, grid=(4,), in_specs=[pl.BlockSpec((2, 256,...  5.89 us
    ppermute x1, starting transfers between devices, shards(): dens_prev = lax.ppermute(density[960:1024], 'space', to_next)  4.93 us
  transfers between devices with their start and end apart: 6, of which 1 were waited for; matrix products, arithmetic and copies ran while one was open for 5% of the time, Pallas kernels for 37%

profile of v1, /device:TPU:0, one launch (start us, length us, event | category | flops | bytes accessed | tf_op | source)
XLA Modules:
  0.0 197.3 jit_solution(10729823951248304113)
XLA Ops:
  6.5 0.9 constant_dynamic-update-slice_fusion.2
  7.5 0.8 constant_dynamic-update-slice_fusion.1
  8.2 0.9 constant_dynamic-update-slice_fusion
  9.2 0.7 slice.24.transfer_ref
  10.0 1.5 fusion.5.basis_ref.basis2_ref
  11.5 5.9 %moments.1 = (bf16[1024,512]{1,0:T(8,128)(2,1)}, bf16[1024,128]{1,0:T(8,128)(2,1)}, bf16[128,128]{1,0:T(8,128)(2,1)}, bf16[16,128]{1,0:T(8,128)(2,1)}, bf16[16,1...) custom-call(f32[2,1024,256]{2,1,0:T(8,128)} %orb_ref.3, ...), custom_call_target="tpu_custom_call" | custom-call | flops 400000000 | bytes 4194304 | tf_op jit(solution)/shard_map/moments/pallas_call | solution.py:90
  17.4 1.4 collective-permute-start.2
  18.8 1.3 collective-permute-start.3
  20.1 0.9 fusion.6
  21.0 4.9 %collective-permute-start = (bf16[64,512]{1,0:T(8,128)(2,1)S(1)}, bf16[64,512]{1,0:T(8,128)(2,1)S(1)}, u32[]{:S(2)}, u32[]{:S(2)}) collective-permute-start(bf16[64,512]{1,0:T(8,128)(2,1)S(1)} %get-tuple-element.32), channel_id=1, source_target_pairs={{0,4},{4,8},{8,12},{12,16},{16,20},{20,24},{24,28},{28,32},{32,36}... | collective-permute-start | bytes 196616 | tf_op jit(solution)/shard_map/ppermute | solution.py:358
  25.9 1.3 collective-permute-start.1
  27.2 0.7 slice_bitcast_fusion
  27.9 0.7 slice.26.coarse_ref
  28.6 0.6 slice.25.pair_ref
  29.2 3.5 %copy.19.coupling_ref = bf16[108,64,64]{2,1,0:T(8,128)(2,1)} copy(bf16[108,64,64]{0,2,1:T(8,128)(2,1)S(1)} %copy-done) | data formatting | bytes 1769472 | tf_op args[8]
  32.7 1.0 copy.17.leaf_list
  33.7 0.7 copy.18.mid_list
  34.5 1.0 copy.16.source_ref
  35.5 30.3 %all-gather = bf16[32,2,128]{2,1,0:T(2,128)(2,1)} all-gather(bf16[1,2,128]{2,1,0:T(2,128)(2,1)S(1)} %slice_bitcast_fusion), channel_id=1, replica_groups=mesh['space'=32,'orb'=4] {'space'}, dimensions={0}, use_global_device_ids=true | all-gather | bytes 16896 | tf_op jit(solution)/shard_map/all_gather | solution.py:362
  67.1 30.1 %near.1 = (f32[1024,512]{1,0:T(8,128)}, bf16[1024,256]{1,0:T(8,128)(2,1)}) custom-call(s32[1024,27]{1,0:T(8,128)} %copy.16.source_ref, bf16[64,512]{1,0:T(8,128)(2,1)} %copy-done.6, bf16[1024,512]{1,0:T(8,128)(2,1)} %get-tuple-element.18.dens_ref, bf16[64,512]{1,0:T(8,128)(2,1)} %copy-done.7, bf16[27,256,256]{2,1,0:T(8,128)(2,1)} %table_ref.1), custom_call_target="tpu_custom_call" | custom-call | flops 15000000512 | bytes 8388608 | tf_op jit(solution)/shard_map/near/pallas_call | solution.py:155
  98.0 34.6 %far.1.far_ref = f32[1280,128]{1,0:T(8,128)} custom-call(s32[1024,108]{1,0:T(8,128)} %copy.17.leaf_list, s32[128,108]{1,0:T(8,128)} %copy.18.mid_list, s32[16,108]{1,0:T(8,128)} %top_list.1, bf16[256,128]{1,0:T(8,128)(2,1)} %copy-done.4, bf16[1024,128]{1,0:T(8,128)(2,1)} %get-tuple-element.22.leaf_ref, bf16[128,128]{1,0:T(8,128)(2,1)} %get-tuple-element.23.mid_ref, ...), custom_call_target="tpu_custom_call" | custom-call | flops 20000000000 | bytes 4194304 | tf_op jit(solution)/shard_map/far/pallas_call | solution.py:230
  132.6 8.3 %tree.1 = (bf16[1024,128]{1,0:T(8,128)(2,1)}, bf16[1024,64]{1,0:T(8,128)(2,1)}) custom-call(bf16[64,128]{1,0:T(8,128)(2,1)} %bitcast.3, bf16[2,128,128]{2,1,0:T(8,128)(2,1)} %slice.25.pair_ref, bf16[4,128,128]{2,1,0:T(8,128)(2,1)} %slice.26.coarse_ref, bf16[8,128,128]{2,1,0:T(8,128)(2,1)} %slice.24.transfer_ref, f32[1280,128]{1,0:T(8,128)} %far.1.far_ref), custom_call_target="tpu_custom_call" | custom-call | flops 600000000 | bytes 2097152 | tf_op jit(solution)/shard_map/tree/pallas_call | solution.py:314
  140.9 44.7 %all-reduce.9.cloned.1.call-done.coeff_sum_ref = bf16[1024,64]{1,0:T(8,128)(2,1)} async-done(((bf16[1024,64]{1,0:T(8,128)(2,1)}), bf16[1024,64]{1,0:T(8,128)(2,1)}) %all-reduce.9.cloned.1.call-update) | async-done | bytes 131088 | tf_op jit(solution)/shard_map/psum | solution.py:368
  185.6 4.8 %relax.1 = f32[2,1024,256]{2,1,0:T(8,128)} custom-call(f32[2,1024,256]{2,1,0:T(8,128)} %orb_ref.3, f32[1024,512]{1,0:T(8,128)} %get-tuple-element.19.near_ref, bf16[1024,128]{1,0:T(8,128)(2,1)} %get-tuple-element.26.coeff_ref, bf16[1024,256]{1,0:T(8,128)(2,1)} %all-reduce.7.cloned.1.call-done.near_sum_ref, ...), custom_call_target="tpu_custom_call" | custom-call | flops 300000000 | bytes 8388608 | tf_op jit(solution)/shard_map/relax/pallas_call | solution.py:335
  (26 shorter events, 2.2 us)
Async XLA Ops:
  6.5 134.3 %all-reduce.7.cloned.1.call-start = ((), (), s32[]{:S(2)}) async-start(), calls=%async_computation | async-start | bytes 1048576 | tf_op jit(solution)/shard_map/psum | solution.py:364
  9.1 20.2 %copy-start = (bf16[108,64,64]{0,2,1:T(8,128)(2,1)S(1)}, bf16[108,64,64]{0,2,1:T(8,128)(2,1)}, u32[]{:S(2)}) copy-start(bf16[108,64,64]{0,2,1:T(8,128)(2,1)} %param.19) | copy-start | bytes 2654212
  17.4 15.3 %copy-start.1 = (s32[1024,108]{0,1:T(8,128)S(1)}, s32[1024,108]{0,1:T(8,128)}, u32[]{:S(2)}) copy-start(s32[1024,108]{0,1:T(8,128)} %param.13) | copy-start | bytes 1327108
  17.4 79.9 %collective-permute-start.2 = (bf16[256,128]{1,0:T(8,128)(2,1)}, bf16[256,128]{1,0:T(8,128)(2,1)S(1)}, u32[]{:S(2)}, u32[]{:S(2)}) collective-permute-start(bf16[256,128]{1,0:T(8,128)(2,1)} %get-tuple-element.21), channel_id=1, source_target_pairs={{0,4},{4,8},{8,12},{12,16},{16,20},{20,24},{24,28},{28,32},{32,36}... | collective-permute-start | bytes 196616 | tf_op jit(solution)/shard_map/ppermute | solution.py:360
  18.8 78.5 %collective-permute-start.3 = (bf16[256,128]{1,0:T(8,128)(2,1)}, bf16[256,128]{1,0:T(8,128)(2,1)S(1)}, u32[]{:S(2)}, u32[]{:S(2)}) collective-permute-start(bf16[256,128]{1,0:T(8,128)(2,1)} %get-tuple-element.25), channel_id=1, source_target_pairs={{4,0},{8,4},{12,8},{16,12},{20,16},{24,20},{28,24},{32,28},{36,32}... | collective-permute-start | bytes 196616 | tf_op jit(solution)/shard_map/ppermute | solution.py:361
  21.0 44.8 %collective-permute-start = (bf16[64,512]{1,0:T(8,128)(2,1)S(1)}, bf16[64,512]{1,0:T(8,128)(2,1)S(1)}, u32[]{:S(2)}, u32[]{:S(2)}) collective-permute-start(bf16[64,512]{1,0:T(8,128)(2,1)S(1)} %get-tuple-element.32), channel_id=1, source_target_pairs={{0,4},{4,8},{8,12},{12,16},{16,20},{20,24},{24,28},{28,32},{32,36}... | collective-permute-start | bytes 196616 | tf_op jit(solution)/shard_map/ppermute | solution.py:358
  25.9 39.9 %collective-permute-start.1 = (bf16[64,512]{1,0:T(8,128)(2,1)S(1)}, bf16[64,512]{1,0:T(8,128)(2,1)S(1)}, u32[]{:S(2)}, u32[]{:S(2)}) collective-permute-start(bf16[64,512]{1,0:T(8,128)(2,1)S(1)} %get-tuple-element.31), channel_id=1, source_target_pairs={{4,0},{8,4},{12,8},{16,12},{20,16},{24,20},{28,24},{32,28},{36,32}... | collective-permute-start | bytes 196616 | tf_op jit(solution)/shard_map/ppermute | solution.py:359
  27.9 5.8 %copy-start.3 = (s32[128,108]{0,1:T(8,128)S(1)}, s32[128,108]{0,1:T(8,128)}, u32[]{:S(2)}) copy-start(s32[128,108]{0,1:T(8,128)} %param.14) | copy-start | bytes 165892
  27.9 6.5 %copy-start.2 = (s32[1024,27]{0,1:T(8,128)S(1)}, s32[1024,27]{0,1:T(8,128)}, u32[]{:S(2)}) copy-start(s32[1024,27]{0,1:T(8,128)} %param.12) | copy-start | bytes 331780
  65.9 0.6 copy-start.6
  66.5 0.6 copy-start.7
  97.3 88.4 %all-reduce.9.cloned.1.call-start = ((), (), s32[]{:S(2)}) async-start(), calls=%async_computation.1 | async-start | bytes 524288 | tf_op jit(solution)/shard_map/psum | solution.py:368
  97.3 0.6 copy-start.4
  97.3 0.7 copy-start.5
Sparse Core Ops, SparseCore 0:
  97.4 43.4 all-reduce.6
  143.2 42.3 all-reduce.8

commit v2 on v1

--- a/solution.py
+++ b/solution.py
@@ -10,6 +10,7 @@
 NN = (((1,), (0,)), ((), ()))
 NT = (((1,), (1,)), ((), ()))
 RELAX_STEP = 0.1
+MESH = pl.DeviceIdType.MESH
 PARAMS = pltpu.CompilerParams(vmem_limit_bytes=56 << 20)
 
 
@@ -27,13 +28,6 @@
 
 def one_hot(column, rows, width):
     return ones_where(iota((rows, width), 1) == column)
-
-
-def twice(matrices):
-    zero = jnp.zeros_like(matrices)
-    top = jnp.concatenate([matrices, zero], axis=-1)
-    low = jnp.concatenate([zero, matrices], axis=-1)
-    return jnp.concatenate([top, low], axis=-2)
 
 
 def octant_picker(parents, half, width):
@@ -54,14 +48,73 @@
     return total.astype(BF)
 
 
+def spread(matrix):
+    zero = jnp.zeros_like(matrix)
+    top = jnp.concatenate([matrix, zero], axis=1)
+    return jnp.concatenate([top, jnp.concatenate([zero, matrix], axis=1)], axis=0)
+
+
+def spread_basis(basis_ref, basis2_ref):
+    basis2_ref[...] = jnp.zeros((128, 512), BF)
+    basis2_ref[0:64, 0:256] = basis_ref[...]
+    basis2_ref[64:128, 256:512] = basis_ref[...]
+
+
 def moments_kernel(
-    orb_ref, basis_ref, transfer_ref, dens_ref, leaf_ref, mid_ref, top_ref, cube_ref, head_ref, tail_ref
+    orb_ref, basis_ref, matrix_ref,
+    dens_ref, leaf_ref, mid_ref, top_ref, dens_prev, dens_next, far_prev, far_next, cubes_ref,
+    basis2_ref, transfer_ref, edge_ref, rim_ref, cube_ref, send, recv, cube_send, cube_recv, own_sem,
 ):
     step = pl.program_id(0)
+    me, orb = lax.axis_index("space"), lax.axis_index("orb")
+    count = lax.axis_size("space")
+    after, before = lax.rem(me + 1, count), lax.rem(me + count - 1, count)
+
+    def halo(number, source, target, device):
+        return pltpu.make_async_remote_copy(
+            src_ref=source,
+            dst_ref=target,
+            send_sem=send.at[number],
+            recv_sem=recv.at[number],
+            device_id=(device, orb),
+            device_id_type=MESH,
+        )
+
+    halos = [
+        halo(0, edge_ref.at[0], dens_next, before),
+        halo(1, edge_ref.at[1], dens_prev, after),
+        halo(2, rim_ref.at[0], far_next, before),
+        halo(3, rim_ref.at[1], far_prev, after),
+    ]
+
+    def cube_copy(other, owner):
+        return pltpu.make_async_remote_copy(
+            src_ref=cube_ref,
+            dst_ref=cubes_ref.at[pl.ds(pl.multiple_of(owner * 16, 16), 16)],
+            send_sem=cube_send.at[other],
+            recv_sem=cube_recv.at[owner],
+            device_id=(other, orb),
+            device_id_type=MESH,
+        )
+
+    @pl.when(step == 0)
+    def _():
+        barrier = pltpu.get_barrier_semaphore()
+
+        def greet(i, _):
+            other = lax.rem(me + i, count)
+            pl.semaphore_signal(barrier, inc=1, device_id=(other, orb), device_id_type=MESH)
+            return 0
+
+        lax.fori_loop(1, count, greet, 0)
+        spread_basis(basis_ref, basis2_ref)
+        for octant in range(8):
+            transfer_ref[octant] = spread(matrix_ref[octant])
+
     for o in range(2):
         values = orb_ref[o]
         dens_ref[:, o * 256 : (o + 1) * 256] = (values * values).astype(BF)
-    leaf = dot(dens_ref[...], basis_ref[...], NT).astype(BF)
+    leaf = dot(dens_ref[...], basis2_ref[...], NT).astype(BF)
     leaf_ref[...] = leaf
     picked = dot(octant_picker(32, 4, 256), leaf).astype(BF)
     mid = merge_up(picked, 32, transfer_ref)
@@ -69,50 +122,98 @@
 
     @pl.when(step == 0)
     def _():
-        head_ref[0:192, :] = leaf[0:192]
+        rim_ref[0, 0:192, :] = leaf[0:192]
+        edge_ref[0] = dens_ref[0:64, :]
+        pl.semaphore_wait(pltpu.get_barrier_semaphore(), count - 1)
+        halos[0].start()
 
     @pl.when(step == 3)
     def _():
-        tail_ref[0:192, :] = leaf[64:256]
+        edge_ref[1] = dens_ref[192:256, :]
+        halos[1].start()
+        rim_ref[1, 0:192, :] = leaf[64:256]
         mids = mid_ref[...]
         top = merge_up(dot(octant_picker(16, 2, 128), mids).astype(BF), 16, transfer_ref)
         top_ref[...] = top
+        rim_ref[0, 192:240, :] = mids[0:48]
+        rim_ref[1, 192:240, :] = mids[80:128]
+        rim_ref[0, 240:256, :] = top
+        rim_ref[1, 240:256, :] = top
+        halos[2].start()
+        halos[3].start()
         cube_ref[...] = merge_up(dot(octant_picker(16, 1, 16), top).astype(BF), 16, transfer_ref)
-        head_ref[192:240, :] = mids[0:48]
-        tail_ref[192:240, :] = mids[80:128]
-        head_ref[240:256, :] = top
-        tail_ref[240:256, :] = top
-
-
-def moments(orbitals, basis2, transfer2):
+
+        def send_cube(i, _):
+            cube_copy(lax.rem(me + i, count), me).start()
+            return 0
+
+        lax.fori_loop(1, count, send_cube, 0)
+        own = pltpu.make_async_copy(
+            cube_ref, cubes_ref.at[pl.ds(pl.multiple_of(me * 16, 16), 16)], own_sem
+        )
+        own.start()
+        own.wait()
+        for copy in halos:
+            copy.wait()
+
+        def wait_cube(i, _):
+            other = lax.rem(me + i, count)
+            cube_copy(other, me).wait_send()
+            cube_copy(other, other).wait_recv()
+            return 0
+
+        lax.fori_loop(1, count, wait_cube, 0)
+
+
+def moments(orbitals, basis, transfer):
     whole = lambda *shape: pl.BlockSpec(shape, lambda c: (0,) * len(shape))
     shape = lambda *s: jax.ShapeDtypeStruct(s, BF)
+    landing = pl.BlockSpec(memory_space=pl.ANY)
+    count = lax.axis_size("space")
     return pl.pallas_call(
         moments_kernel,
         grid=(4,),
-        in_specs=[pl.BlockSpec((2, 256, 256), lambda c: (0, c, 0)), whole(128, 512), whole(8, 128, 128)],
+        in_specs=[pl.BlockSpec((2, 256, 256), lambda c: (0, c, 0)), whole(64, 256), whole(8, 64, 64)],
         out_specs=[
             pl.BlockSpec((256, 512), lambda c: (c, 0)),
             pl.BlockSpec((256, 128), lambda c: (c, 0)),
             whole(128, 128),
             whole(16, 128),
-            whole(16, 128),
-            whole(256, 128),
-            whole(256, 128),
+            landing,
+            landing,
+            landing,
+            landing,
+            landing,
         ],
         out_shape=[
             shape(1024, 512),
             shape(1024, 128),
             shape(128, 128),
             shape(16, 128),
-            shape(16, 128),
+            shape(64, 512),
+            shape(64, 512),
             shape(256, 128),
             shape(256, 128),
-        ],
-        compiler_params=PARAMS,
+            shape(count * 16, 128),
+        ],
+        scratch_shapes=[
+            pltpu.VMEM((128, 512), BF),
+            pltpu.VMEM((8, 128, 128), BF),
+            pltpu.VMEM((2, 64, 512), BF),
+            pltpu.VMEM((2, 256, 128), BF),
+            pltpu.VMEM((16, 128), BF),
+            pltpu.SemaphoreType.DMA((4,)),
+            pltpu.SemaphoreType.DMA((4,)),
+            pltpu.SemaphoreType.DMA((count,)),
+            pltpu.SemaphoreType.DMA((count,)),
+            pltpu.SemaphoreType.DMA,
+        ],
+        compiler_params=pltpu.CompilerParams(
+            vmem_limit_bytes=40 << 20, collective_id=0, has_side_effects=True
+        ),
         cost_estimate=pl.CostEstimate(flops=400_000_000, bytes_accessed=4 << 20, transcendentals=0),
         name="moments",
-    )(orbitals, basis2, transfer2)
+    )(orbitals, basis, transfer)
 
 
 def near_kernel(
@@ -257,8 +358,22 @@
     )(far_leaf, far_mid, far_top, prev, leaf, mid, top, after, coupling)
 
 
-def tree_kernel(cube_ref, pair_ref, coarse_ref, transfer_ref, far_ref, coeff_ref, sum_ref):
-    device = lax.axis_index("space")
+def tree_kernel(
+    cube_ref, pair_in, coarse_in, transfer_in, far_ref,
+    coeff_ref, sum_ref,
+    pair_ref, coarse_ref, transfer_ref, part_ref, other_ref, send, recv,
+):
+    device, orb = lax.axis_index("space"), lax.axis_index("orb")
+    orbs = lax.axis_size("orb")
+    barrier = pltpu.get_barrier_semaphore()
+    for away in range(1, orbs):
+        other = lax.rem(orb + away, orbs)
+        pl.semaphore_signal(barrier, inc=1, device_id=(device, other), device_id_type=MESH)
+    for given, kept in ((pair_in, pair_ref), (coarse_in, coarse_ref), (transfer_in, transfer_ref)):
+        for i in range(given.shape[0]):
+            kept[i] = spread(given[i])
+    row, col = iota((64, cube_ref.shape[0]), 0), iota((64, cube_ref.shape[0]), 1)
+    cubes = dot(ones_where(col == 16 * (row // 2) + row % 2), cube_ref[...]).astype(BF)
     row, col = iota((64, 64), 0), iota((64, 64), 1)
     child = [ones_where(col == 2 * row + p) for p in range(2)]
     mother = [ones_where((col == row // 2) & (row % 2 == p)) for p in range(2)]
@@ -268,7 +383,7 @@
         ones_where(col == row + 2),
         ones_where((col == row + 3) & (row % 2 == 0)),
     ]
-    levels = [cube_ref[...]]
+    levels = [cubes]
     for _ in range(6):
         total = None
         for p in range(2):
@@ -287,13 +402,14 @@
                 total = total + dot(dot(mother[p], coeffs).astype(BF), pair_ref[p], NT)
         coeffs = total.astype(BF)
 
-    def split_down(coeffs, parents, children, half, first):
-        row, col = iota((children, parents), 0), iota((children, parents), 1)
+    def split_down(coeffs, children, half, first, start, rows):
+        parents = coeffs.shape[0]
         side = 2 * half
+        row, col = iota((rows, parents), 0) + start, iota((rows, parents), 1)
         z, y, x = row // (side * side), (row // side) % side, row % side
         parent = ((z // 2) * half + y // 2) * half + x // 2 + first
         pulled = dot(ones_where(col == parent), coeffs).astype(BF)
-        r = iota((children, 128), 0)
+        r = iota((rows, 128), 0) + start
         octant = 4 * ((r // (side * side)) % 2) + 2 * ((r // side) % 2) + r % 2
         total = None
         for o in range(8):
@@ -301,72 +417,111 @@
             total = part if total is None else total + part
         return total
 
-    top = 0.25 * far_ref[1152:1168] + split_down(coeffs, 64, 16, 1, 2 * device)
-    mid = 0.5 * far_ref[1024:1152] + split_down(top.astype(BF), 16, 128, 2, 0)
-    leaf = far_ref[0:1024] + split_down(mid.astype(BF), 128, 1024, 4, 0)
-    leaf = leaf.astype(BF)
-    coeff_ref[...] = leaf
-    wide = leaf.astype(F32)
-    sum_ref[...] = (wide[:, :64] + wide[:, 64:]).astype(BF)
-
-
-def tree_down(cubes, pair2, coarse2, transfer2, far):
+    top = 0.25 * far_ref[1152:1168] + split_down(coeffs, 16, 1, 2 * device, 0, 16)
+    mid = 0.5 * far_ref[1024:1152] + split_down(top.astype(BF), 128, 2, 0, 0, 128)
+    mid = mid.astype(BF)
+    pl.semaphore_wait(barrier, orbs - 1)
+
+    def copies(chunk):
+        rows = pl.ds(chunk * 128, 128)
+        found = []
+        for away in range(1, orbs):
+            found.append(
+                pltpu.make_async_remote_copy(
+                    src_ref=part_ref.at[rows],
+                    dst_ref=other_ref.at[away - 1, rows],
+                    send_sem=send.at[away - 1, chunk],
+                    recv_sem=recv.at[away - 1, chunk],
+                    device_id=(device, lax.rem(orb + away, orbs)),
+                    device_id_type=MESH,
+                )
+            )
+        return found
+
+    left = iota((128, 128), 1) < 64
+    for chunk in range(4):
+        rows = slice(chunk * 256, (chunk + 1) * 256)
+        leaf = far_ref[rows] + split_down(mid, 1024, 4, 0, chunk * 256, 256)
+        leaf = leaf.astype(BF)
+        coeff_ref[rows] = leaf
+        wide = leaf.astype(F32)
+        wide = wide + pltpu.roll(wide, 64, 1)
+        packed = jnp.where(left, wide[0:128], wide[128:256])
+        part_ref[chunk * 128 : (chunk + 1) * 128, :] = packed.astype(BF)
+        for copy in copies(chunk):
+            copy.start()
+    for chunk in range(4):
+        for copy in copies(chunk):
+            copy.wait()
+        rows = slice(chunk * 128, (chunk + 1) * 128)
+        total = part_ref[rows].astype(F32)
+        for away in range(1, orbs):
+            total = total + other_ref[away - 1, rows].astype(F32)
+        sum_ref[rows] = total.astype(BF)
+
+
+def tree_down(cubes, pair, coarse, transfer, far):
+    orbs = lax.axis_size("orb")
     return pl.pallas_call(
         tree_kernel,
-        out_shape=[jax.ShapeDtypeStruct((1024, 128), BF), jax.ShapeDtypeStruct((1024, 64), BF)],
-        compiler_params=PARAMS,
+        out_shape=[jax.ShapeDtypeStruct((1024, 128), BF), jax.ShapeDtypeStruct((512, 128), BF)],
+        scratch_shapes=[
+            pltpu.VMEM((2, 128, 128), BF),
+            pltpu.VMEM((4, 128, 128), BF),
+            pltpu.VMEM((8, 128, 128), BF),
+            pltpu.VMEM((512, 128), BF),
+            pltpu.VMEM((orbs - 1, 512, 128), BF),
+            pltpu.SemaphoreType.DMA((orbs - 1, 4)),
+            pltpu.SemaphoreType.DMA((orbs - 1, 4)),
+        ],
+        compiler_params=pltpu.CompilerParams(
+            vmem_limit_bytes=40 << 20, collective_id=1, has_side_effects=True
+        ),
         cost_estimate=pl.CostEstimate(flops=600_000_000, bytes_accessed=2 << 20, transcendentals=0),
         name="tree",
-    )(cubes, pair2, coarse2, transfer2, far)
-
-
-def relax_kernel(orb_ref, near_ref, coeff_ref, near_sum_ref, coeff_sum_ref, basis2_ref, basis_ref, out_ref):
+    )(cubes, pair, coarse, transfer, far)
+
+
+def relax_kernel(orb_ref, near_ref, coeff_ref, near_sum_ref, coeff_sum_ref, basis_ref, out_ref, basis2_ref):
+    @pl.when(pl.program_id(0) == 0)
+    def _():
+        spread_basis(basis_ref, basis2_ref)
+
     potential = near_ref[...] + dot(coeff_ref[...], basis2_ref[...])
-    hartree = near_sum_ref[...].astype(F32) + dot(coeff_sum_ref[...], basis_ref[...])
+    both = dot(coeff_sum_ref[...], basis2_ref[...])
+    hartree = jnp.concatenate([both[:, :256], both[:, 256:]], axis=0) + near_sum_ref[...].astype(F32)
     for o in range(2):
         values = orb_ref[o]
         out_ref[o] = values - RELAX_STEP * (hartree - potential[:, o * 256 : (o + 1) * 256]) * values
 
 
-def relax(orbitals, near, coeffs, near_sum, coeff_sum, basis2, basis):
+def relax(orbitals, near, coeffs, near_sum, coeff_sum, basis):
     whole = lambda *shape: pl.BlockSpec(shape, lambda c: (0,) * len(shape))
     rows = lambda *shape: pl.BlockSpec(shape, lambda c: (c, 0))
     block = pl.BlockSpec((2, 256, 256), lambda c: (0, c, 0))
     return pl.pallas_call(
         relax_kernel,
         grid=(4,),
-        in_specs=[block, rows(256, 512), rows(256, 128), rows(256, 256), rows(256, 64), whole(128, 512), whole(64, 256)],
+        in_specs=[block, rows(256, 512), rows(256, 128), rows(256, 256), rows(128, 128), whole(64, 256)],
         out_specs=block,
         out_shape=jax.ShapeDtypeStruct((2, 1024, 256), F32),
+        scratch_shapes=[pltpu.VMEM((128, 512), BF)],
         compiler_params=PARAMS,
         cost_estimate=pl.CostEstimate(flops=300_000_000, bytes_accessed=8 << 20, transcendentals=0),
         name="relax",
-    )(orbitals, near, coeffs, near_sum, coeff_sum, basis2, basis)
+    )(orbitals, near, coeffs, near_sum, coeff_sum, basis)
 
 
 def shards(
     orbitals, near_source, far_leaf, far_mid, far_top, leaf_basis, near_table, transfer, coupling, pair_transfer,
     coarse_coupling,
 ):
-    count = lax.axis_size("space")
-    to_next = [(i, i + 1) for i in range(count - 1)]
-    to_prev = [(i + 1, i) for i in range(count - 1)]
-    basis2 = twice(leaf_basis)
-    small = twice(jnp.concatenate([transfer, pair_transfer, coarse_coupling], axis=0))
-    transfer2, pair2, coarse2 = small[0:8], small[8:10], small[10:14]
-    density, leaf, mid, top, cube, head, tail = moments(orbitals, basis2, transfer2)
-    dens_prev = lax.ppermute(density[960:1024], "space", to_next)
-    dens_next = lax.ppermute(density[0:64], "space", to_prev)
-    far_prev = lax.ppermute(tail, "space", to_next)
-    far_next = lax.ppermute(head, "space", to_prev)
-    cubes = lax.all_gather(cube[0:2], "space", axis=0, tiled=True)
+    density, leaf, mid, top, dens_prev, dens_next, far_prev, far_next, cubes = moments(orbitals, leaf_basis, transfer)
     near, near_part = near_field(near_source, dens_prev, density, dens_next, near_table)
     near_sum = lax.psum(near_part, "orb")
     far = far_sums(far_leaf, far_mid, far_top, far_prev, leaf, mid, top, far_next, coupling)
-    coeffs, coeff_part = tree_down(cubes, pair2, coarse2, transfer2, far)
-    near_sum, coeff_part = lax.optimization_barrier((near_sum, coeff_part))
-    coeff_sum = lax.psum(coeff_part, "orb")
-    return relax(orbitals, near, coeffs, near_sum, coeff_sum, basis2, leaf_basis)
+    coeffs, coeff_sum = tree_down(cubes, pair_transfer, coarse_coupling, transfer, far)
+    return relax(orbitals, near, coeffs, near_sum, coeff_sum, leaf_basis)
 
 
 def solution(mesh):

time: 198 us -> 134 us (0.68)
  waiting for transfers between devices: 44.8 us -> 0.02 us
  blocking collectives: 30.3 us -> 0 us
  Pallas kernels: 83.6 us -> 102 us
  starting transfers between devices: 8.98 us -> 0.01 us
  local copies, waits for them, and re-layouts: 14.3 us -> 18.2 us
    psum x1 -> x0, waiting for transfers between devices: 44.7 us -> none  [shards(): coeff_sum = lax.psum(coeff_part, 'orb')]
    all_gather x1 -> x0, blocking collectives: 30.3 us -> none  [shards(): cubes = lax.all_gather(cube[0:2], 'space', axis=0, tiled=True)]
    pallas_call x1, Pallas kernels: 5.89 us -> 15.9 us  [moments(): pl.pallas_call(moments_kernel, grid=(4,), in_specs=[pl.BlockSpec((2, 256,...]
    ppermute x4 -> x0, starting transfers between devices: 8.93 us -> none  [the longest x1 4.93 us: shards(): dens_prev = lax.ppermute(density[960:1024], 'space', to_next)]
    pallas_call x1, Pallas kernels: 8.27 us -> 16.1 us  [tree_down(): pl.pallas_call(tree_kernel, out_shape=[jax.ShapeDtypeStruct((1024, 128),...]
    unnamed x23 -> x44, local copies, waits for them, and re-layouts: 10.6 us -> 18.2 us
    slice x4 -> x0, local copies, waits for them, and re-layouts: 2.91 us -> none  [the longest x3 2.03 us: shards(): transfer2, pair2, coarse2 = (small[0:8], small[8:10], small[10:14])]
  transfers between devices with their start and end apart: 6 -> 1, of which waited for: 1 -> 0; matrix products, arithmetic and copies ran while one was open for 5% -> 4% of each run, Pallas kernels for 37% -> 38%
where the time goes in v2:
time: 134 us; the launch traced here: 133 us
  Pallas kernels  102 us (76%)
  local copies, waits for them, and re-layouts  18.2 us (14%)
  between operations  13.5 us (10%)
    pallas_call x1, Pallas kernels, far_sums(): pl.pallas_call(far_kernel, grid=(5,), in_specs=[pl.BlockSpec((256, 108),...  34.8 us
    pallas_call x1, Pallas kernels, near_field(): pl.pallas_call(near_kernel, grid=(4,), in_specs=[rows(256, 27), whole(64,...  30.2 us
    unnamed x44, local copies, waits for them, and re-layouts  18.2 us
    pallas_call x1, Pallas kernels, tree_down(): pl.pallas_call(tree_kernel, out_shape=[jax.ShapeDtypeStruct((1024, 128),...  16.1 us
    pallas_call x1, Pallas kernels, moments(): pl.pallas_call(moments_kernel, grid=(4,), in_specs=[pl.BlockSpec((2, 256,...  15.9 us
    pallas_call x1, Pallas kernels, relax(): pl.pallas_call(relax_kernel, grid=(4,), in_specs=[block, rows(256, 512),...  4.79 us
  transfers between devices with their start and end apart: 1, of which 0 were waited for; matrix products, arithmetic and copies ran while one was open for 4% of the time, Pallas kernels for 38%

profile of v2, /device:TPU:0, one launch (start us, length us, event | category | flops | bytes accessed | tf_op | source)
XLA Modules:
  0.0 133.4 jit_solution(13188174076579599306)
XLA Ops:
  6.5 1.9 %copy.12.source_ref = s32[1024,27]{1,0:T(8,128)} copy(s32[1024,27]{0,1:T(8,128)} %param.12) | data formatting | bytes 221184 | tf_op args[1]
  8.4 1.6 %copy-done = f32[2,1024,256]{2,1,0:T(8,128)S(1)} copy-done((f32[2,1024,256]{2,1,0:T(8,128)S(1)}, f32[2,1024,256]{2,1,0:T(8,128)}, u32[]{:S(2)}) %copy-start) | copy-done | bytes 2097176
  10.0 0.8 copy-done.3
  10.8 0.9 copy-done.4
  11.7 15.9 %moments.1 = (bf16[1024,512]{1,0:T(8,128)(2,1)S(1)}, bf16[1024,128]{1,0:T(8,128)(2,1)S(1)}, bf16[128,128]{1,0:T(8,128)(2,1)S(1)}, bf16[16,128]{1,0:T(8,128)(2,1)...) custom-call(f32[2,1024,256]{2,1,0:T(8,128)S(1)} %copy-done, ...), custom_call_target="tpu_custom_call" | custom-call | flops 400000000 | bytes 4194304 | tf_op jit(solution)/shard_map/moments/pallas_call | solution.py:173
  27.6 1.0 copy-done.6
  28.6 0.7 copy-done.7
  29.3 0.6 copy-done.9
  29.9 0.6 copy-done.10
  30.5 0.6 copy-done.11
  31.1 0.6 copy-done.12
  31.8 0.6 copy-done.14
  32.4 0.6 copy-done.15
  32.9 30.2 %near.1 = (f32[1024,512]{1,0:T(8,128)}, bf16[1024,256]{1,0:T(8,128)(2,1)}) custom-call(s32[1024,27]{1,0:T(8,128)} %copy.12.source_ref, bf16[64,512]{1,0:T(8,128)(2,1)} %copy-done.11, bf16[1024,512]{1,0:T(8,128)(2,1)} %copy-done.6, bf16[64,512]{1,0:T(8,128)(2,1)} %copy-done.12, bf16[27,256,256]{2,1,0:T(8,128)(2,1)} %table_ref.1), custom_call_target="tpu_custom_call" | custom-call | flops 15000000512 | bytes 8388608 | tf_op jit(solution)/shard_map/near/pallas_call | solution.py:256
  63.2 0.0 all-reduce.2.cloned.1.call-update
  63.2 3.5 %copy.15.coupling_ref = bf16[108,64,64]{2,1,0:T(8,128)(2,1)} copy(bf16[108,64,64]{0,2,1:T(8,128)(2,1)S(1)} %copy-done.17) | data formatting | bytes 1769472 | tf_op args[8]
  66.7 1.0 copy.13.leaf_list
  67.7 0.7 copy.14.mid_list
  68.4 34.8 %far.1.far_ref = f32[1280,128]{1,0:T(8,128)} custom-call(s32[1024,108]{1,0:T(8,128)} %copy.13.leaf_list, s32[128,108]{1,0:T(8,128)} %copy.14.mid_list, s32[16,108]{1,0:T(8,128)} %top_list.1, bf16[256,128]{1,0:T(8,128)(2,1)} %copy-done.9, bf16[1024,128]{1,0:T(8,128)(2,1)} %copy-done.7, bf16[128,128]{1,0:T(8,128)(2,1)} %copy-done.14, ...), custom_call_target="tpu_custom_call" | custom-call | flops 20000000000 | bytes 4194304 | tf_op jit(solution)/shard_map/far/pallas_call | solution.py:331
  103.2 1.1 copy-done.16
  104.3 16.1 %tree.1 = (bf16[1024,128]{1,0:T(8,128)(2,1)S(1)}, bf16[512,128]{1,0:T(8,128)(2,1)S(1)}) custom-call(bf16[512,128]{1,0:T(8,128)(2,1)S(1)} %get-tuple-element.22.cube_ref, bf16[2,64,64]{2,1,0:T(8,128)(2,1)S(1)} %copy-done.13, bf16[4,64,64]{2,1,0:T(8,128)(2,1)S(1)} %copy-done.8, bf16[8,64,64]{2,1,0:T(8,128)(2,1)S(1)} %copy-done.5, f32[1280,128]{1,0:T(8,128)S(1)} %copy-done.16), custom_call_target="tpu_custom_call" | custom-call | flops 600000000 | bytes 2097152 | tf_op jit(solution)/shard_map/tree/pallas_call | solution.py:465
  120.4 0.7 copy-done.1
  121.1 0.7 copy-done.2
  121.8 4.8 %relax.1 = f32[2,1024,256]{2,1,0:T(8,128)} custom-call(f32[2,1024,256]{2,1,0:T(8,128)} %orb_ref.3, f32[1024,512]{1,0:T(8,128)} %get-tuple-element.21.near_ref, bf16[1024,128]{1,0:T(8,128)(2,1)} %copy-done.1, bf16[1024,256]{1,0:T(8,128)(2,1)} %all-reduce.2.cloned.1.call-done.near_sum_ref, bf16[512,128]{1,0:T(8,128)(2,1)} %copy-done.2, bf16[64,256]{1,0:T(8,128)(2,1)} %basis_ref.3), custom_call_target="tpu_custom_call" | custom-call | flops 300000000 | bytes 8388608 | tf_op jit(solution)/shard_map/relax/pallas_call | solution.py:502
  (28 shorter events, 0.1 us)
Async XLA Ops:
  6.5 115.3 %all-reduce.2.cloned.1.call-start = ((), (), s32[]{:S(2)}) async-start(), calls=%async_computation | async-start | bytes 1048576 | tf_op jit(solution)/shard_map/psum | solution.py:521
  8.4 1.6 %copy-start = (f32[2,1024,256]{2,1,0:T(8,128)S(1)}, f32[2,1024,256]{2,1,0:T(8,128)}, u32[]{:S(2)}) copy-start(f32[2,1024,256]{2,1,0:T(8,128)} %orb_ref.3) | copy-start | bytes 6291460
  10.0 0.8 copy-start.3
  10.8 0.9 copy-start.4
  27.6 1.0 copy-start.6
  28.6 0.7 copy-start.7
  29.3 0.6 copy-start.9
  29.9 0.6 copy-start.10
  30.5 0.6 copy-start.11
  31.1 0.6 copy-start.12
  31.8 0.6 copy-start.14
  32.4 0.6 copy-start.15
  32.9 30.2 %copy-start.17 = (bf16[108,64,64]{0,2,1:T(8,128)(2,1)S(1)}, bf16[108,64,64]{0,2,1:T(8,128)(2,1)}, u32[]{:S(2)}) copy-start(bf16[108,64,64]{0,2,1:T(8,128)(2,1)} %param.19) | copy-start | bytes 2654212
  63.1 3.5 %copy-start.18 = (s32[1024,108]{0,1:T(8,128)S(1)}, s32[1024,108]{0,1:T(8,128)}, u32[]{:S(2)}) copy-start(s32[1024,108]{0,1:T(8,128)} %param.13) | copy-start | bytes 1327108
  63.1 4.5 %copy-start.19 = (s32[128,108]{0,1:T(8,128)S(1)}, s32[128,108]{0,1:T(8,128)}, u32[]{:S(2)}) copy-start(s32[128,108]{0,1:T(8,128)} %param.14) | copy-start | bytes 165892
  68.4 34.8 %copy-start.5 = (bf16[8,64,64]{2,1,0:T(8,128)(2,1)S(1)}, bf16[8,64,64]{2,1,0:T(8,128)(2,1)}, u32[]{:S(2)}) copy-start(bf16[8,64,64]{2,1,0:T(8,128)(2,1)} %transfer_in.1) | copy-start | bytes 196612
  68.4 34.8 %copy-start.8 = (bf16[4,64,64]{2,1,0:T(8,128)(2,1)S(1)}, bf16[4,64,64]{2,1,0:T(8,128)(2,1)}, u32[]{:S(2)}) copy-start(bf16[4,64,64]{2,1,0:T(8,128)(2,1)} %coarse_in.1) | copy-start | bytes 98308
  68.4 34.8 %copy-start.13 = (bf16[2,64,64]{2,1,0:T(8,128)(2,1)S(1)}, bf16[2,64,64]{2,1,0:T(8,128)(2,1)}, u32[]{:S(2)}) copy-start(bf16[2,64,64]{2,1,0:T(8,128)(2,1)} %pair_in.1) | copy-start | bytes 49156
  103.2 1.1 copy-start.16
  120.4 0.7 copy-start.1
  121.1 0.7 copy-start.2
Sparse Core Ops, SparseCore 0:
  63.3 42.1 all-reduce.1

commit v3 on v1

v3 whole, which is shorter than its diff:
```python
import jax
import jax.numpy as jnp
from jax import lax
from jax.experimental import pallas as pl
from jax.experimental.pallas import tpu as pltpu
from jax.sharding import PartitionSpec as P

BF = jnp.bfloat16
F32 = jnp.float32
NN = (((1,), (0,)), ((), ()))
NT = (((1,), (1,)), ((), ()))
RELAX_STEP = 0.1
MESH = pl.DeviceIdType.MESH


def dot(a, b, dims=NN):
    return lax.dot_general(a, b, dims, preferred_element_type=F32)


def iota(shape, dim):
    return lax.broadcasted_iota(jnp.int32, shape, dim)


def ones_where(mask):
    return jnp.where(mask, 1.0, 0.0).astype(BF)


def one_hot(column, rows, width):
    return ones_where(iota((rows, width), 1) == column)


def octant_picker(parents, half, width):
    row, col = iota((8 * parents, width), 0), iota((8 * parents, width), 1)
    octant, b = row // parents, row % parents
    z, y, x = b // (half * half), (b // half) % half, b % half
    dz, dy, dx = octant // 4, (octant // 2) % 2, octant % 2
    side = 2 * half
    child = ((2 * z + dz) * side + 2 * y + dy) * side + 2 * x + dx
    return ones_where(child == col)


def merge_up(picked, parents, transfer_ref):
    total = None
    for octant in range(8):
        part = dot(picked[octant * parents : (octant + 1) * parents], transfer_ref[octant])
        total = part if total is None else total + part
    return total.astype(BF)


def spread(matrix):
    zero = jnp.zeros_like(matrix)
    top = jnp.concatenate([matrix, zero], axis=1)
    return jnp.concatenate([top, jnp.concatenate([zero, matrix], axis=1)], axis=0)


def spread_basis(basis_ref, basis2_ref):
    basis2_ref[...] = jnp.zeros((128, 512), BF)
    basis2_ref[0:64, 0:256] = basis_ref[...]
    basis2_ref[64:128, 256:512] = basis_ref[...]


def step_kernel(
    orb_hbm, near_list, leaf_list, mid_list, top_list, basis_ref, table_hbm, transfer_in, coupling_hbm, pair_in, coarse_in,
    out_hbm,
    orb_ref, table_ref, coupling_ref, dens_ref, leaf_ref, mid_ref, top_ref, cube_ref, basis2_ref, transfer_ref, pair_ref,
    coarse_ref, weight_ref, hot_ref, near_pick, far_pick, near_ref, near_part, near_other, coeff_ref, coeff_part, coeff_other,
    load_sem, out_sem, halo_send, halo_recv, cube_send, cube_recv, near_send, near_recv, coeff_send, coeff_recv,
):
    me, orb = lax.axis_index("space"), lax.axis_index("orb")
    count, orbs = lax.axis_size("space"), lax.axis_size("orb")
    after, before = lax.rem(me + 1, count), lax.rem(me + count - 1, count)
    barrier = pltpu.get_barrier_semaphore()

    def greet(i, _):
        other = lax.rem(me + i, count)
        pl.semaphore_signal(barrier, inc=1, device_id=(other, orb), device_id_type=MESH)
        return 0

    lax.fori_loop(1, count, greet, 0)
    for away in range(1, orbs):
        other = lax.rem(orb + away, orbs)
        pl.semaphore_signal(barrier, inc=1, device_id=(me, other), device_id_type=MESH)

    def rows_of(c, size):
        return pl.ds(pl.multiple_of(c * size, size), size)

    def load_orbitals(c):
        rows = rows_of(c, 256)
        return pltpu.make_async_copy(orb_hbm.at[:, rows], orb_ref.at[:, rows], load_sem.at[c])

    load_table = pltpu.make_async_copy(table_hbm, table_ref, load_sem.at[4])
    load_coupling = pltpu.make_async_copy(coupling_hbm, coupling_ref, load_sem.at[5])
    for c in range(4):
        load_orbitals(c).start()
    load_table.start()
    load_coupling.start()

    spread_basis(basis_ref, basis2_ref)
    for given, kept in ((pair_in, pair_ref), (coarse_in, coarse_ref), (transfer_in, transfer_ref)):
        for i in range(given.shape[0]):
            kept[i] = spread(given[i])
    mid_ref[224:256, :] = jnp.zeros((32, 128), BF)
    top_ref[48:128, :] = jnp.zeros((80, 128), BF)

    def moments_chunk(c, _):
        load_orbitals(c).wait()
        rows = rows_of(c, 256)
        inner = pl.ds(pl.multiple_of(64 + c * 256, 64), 256)
        for o in range(2):
            values = orb_ref[o, rows, :]
            dens_ref[inner, o * 256 : (o + 1) * 256] = (values * values).astype(BF)
        leaf = dot(dens_ref[inner, :], basis2_ref[...], NT).astype(BF)
        leaf_ref[pl.ds(pl.multiple_of(192 + c * 256, 64), 256), :] = leaf
        picked = dot(octant_picker(32, 4, 256), leaf).astype(BF)
        mid_ref[pl.ds(pl.multiple_of(48 + c * 32, 16), 32), :] = merge_up(picked, 32, transfer_ref)
        return 0

    lax.fori_loop(0, 4, moments_chunk, 0)
    pl.semaphore_wait(barrier, count - 1 + orbs - 1)

    def halo(number, ref, head, tail, rows, ahead):
        source, target, device = (tail, 0, after) if ahead else (head, tail + rows, before)
        return pltpu.make_async_remote_copy(
            src_ref=ref.at[pl.ds(source, rows)],
            dst_ref=ref.at[pl.ds(target, rows)],
            send_sem=halo_send.at[number],
            recv_sem=halo_recv.at[number],
            device_id=(device, orb),
            device_id_type=MESH,
        )

    halos = []
    for ref, head, tail, rows in (
        (dens_ref, 64, 1024, 64),
        (leaf_ref, 192, 1024, 192),
        (mid_ref, 48, 128, 48),
        (top_ref, 16, 16, 16),
    ):
        for ahead in (False, True):
            halos.append(halo(len(halos), ref, head, tail, rows, ahead))
    for copy in halos[0:6]:
        copy.start()
    top = merge_up(dot(octant_picker(16, 2, 128), mid_ref[48:176, :]).astype(BF), 16, transfer_ref)
    top_ref[16:32, :] = top
    for copy in halos[6:8]:
        copy.start()
    cube_ref[rows_of(me, 16), :] = merge_up(
        dot(octant_picker(16, 1, 16), top).astype(BF), 16, transfer_ref
    )

    def cube_copy(other, owner):
        block = cube_ref.at[rows_of(owner, 16)]
        return pltpu.make_async_remote_copy(
            src_ref=block,
            dst_ref=block,
            send_sem=cube_send.at[other],
            recv_sem=cube_recv.at[owner],
            device_id=(other, orb),
            device_id_type=MESH,
        )

    def send_cube(i, _):
        cube_copy(lax.rem(me + i, count), me).start()
        return 0

    lax.fori_loop(1, count, send_cube, 0)

    def to_orbs(part, landing, send, recv, c, size):
        rows = rows_of(c, size)
        return [
            pltpu.make_async_remote_copy(
                src_ref=part.at[rows],
                dst_ref=landing.at[away - 1, rows],
                send_sem=send.at[away - 1, c],
                recv_sem=recv.at[away - 1, c],
                device_id=(me, lax.rem(orb + away, orbs)),
                device_id_type=MESH,
            )
            for away in range(1, orbs)
        ]

    load_table.wait()

    def near_chunk(i, _):
        c = lax.rem(i + 1, 4)

        @pl.when(i == 2)
        def _():
            for copy in halos[0:2]:
                copy.wait()

        for part in range(2):
            base = pl.multiple_of(c * 256 + part * 128, 128)
            place = (near_list[:, pl.ds(base, 128)].T + (64 + 128 * part)) & 255
            for k in range(27):
                hot_ref[k * 128 : (k + 1) * 128, :] = one_hot(place[:, k : k + 1], 128, 256)
            for o in range(2):
                source = dens_ref[pl.ds(base, 256), o * 256 : (o + 1) * 256]
                at = o * 256 + part * 128
                for first in range(0, 27, 9):
                    picked = dot(hot_ref[first * 128 : (first + 9) * 128, :], source).astype(BF)
                    for k in range(9):
                        near_pick[at : at + 128, (first + k) * 256 : (first + k + 1) * 256] = picked[
                            k * 128 : (k + 1) * 128
                        ]
        total = None
        for k in range(27):
            part = dot(near_pick[:, k * 256 : (k + 1) * 256], table_ref[k], NT)
            total = part if total is None else total + part
        rows = rows_of(c, 256)
        near_ref[rows, 0:256] = total[:256]
        near_ref[rows, 256:512] = total[256:]
        near_part[rows, :] = (total[:256] + total[256:]).astype(BF)
        for copy in to_orbs(near_part, near_other, near_send, near_recv, c, 256):
            copy.start()
        return 0

    lax.fori_loop(0, 4, near_chunk, 0)

    load_coupling.wait()
    for k in range(108):
        weight_ref[:, k * 128 : (k + 1) * 128] = spread(coupling_ref[k])
    for copy in halos[2:8]:
        copy.wait()

    def pick(place, rows, at, table):
        width = table.shape[0]
        for k in range(108):
            hot_ref[k * rows : (k + 1) * rows, :width] = one_hot(place[:, k : k + 1], rows, width)
        for first in range(0, 108, 12):
            picked = dot(hot_ref[first * rows : (first + 12) * rows, :width], table).astype(BF)
            for k in range(12):
                far_pick[at : at + rows, (first + k) * 128 : (first + k + 1) * 128] = picked[
                    k * rows : (k + 1) * rows
                ]

    mid_place = mid_list[...].T - (me * 128 - 48)
    pick(mid_place[0:64], 64, 0, mid_ref[...])
    pick(mid_place[64:128], 64, 64, mid_ref[...])
    pick(top_list[...].T - (me * 16 - 16), 16, 128, top_ref[...])
    far = dot(far_pick[0:144, :], weight_ref[...], NT)

    def wait_cube(i, _):
        other = lax.rem(me + i, count)
        cube_copy(other, me).wait_send()
        cube_copy(other, other).wait_recv()
        return 0

    lax.fori_loop(1, count, wait_cube, 0)
    row, col = iota((64, cube_ref.shape[0]), 0), iota((64, cube_ref.shape[0]), 1)
    cubes = dot(ones_where(col == 16 * (row // 2) + row % 2), cube_ref[...]).astype(BF)
    row, col = iota((64, 64), 0), iota((64, 64), 1)
    child = [ones_where(col == 2 * row + p) for p in range(2)]
    mother = [ones_where((col == row // 2) & (row % 2 == p)) for p in range(2)]
    shift = [
        ones_where((col == row - 3) & (row % 2 == 1)),
        ones_where(col == row - 2),
        ones_where(col == row + 2),
        ones_where((col == row + 3) & (row % 2 == 0)),
    ]
    levels = [cubes]
    for _ in range(6):
        total = None
        for p in range(2):
            part = dot(dot(child[p], levels[-1]).astype(BF), pair_ref[p])
            total = part if total is None else total + part
        levels.append(total.astype(BF))
    coeffs = None
    for depth in range(6, -1, -1):
        total = None
        for w in range(4):
            part = dot(dot(shift[w], levels[depth]).astype(BF), coarse_ref[w], NT)
            total = part if total is None else total + part
        total = total * (0.5 ** (3 + depth))
        if coeffs is not None:
            for p in range(2):
                total = total + dot(dot(mother[p], coeffs).astype(BF), pair_ref[p], NT)
        coeffs = total.astype(BF)

    def split_down(coeffs, half, first, start, rows):
        parents = coeffs.shape[0]
        side = 2 * half
        row, col = iota((rows, parents), 0) + start, iota((rows, parents), 1)
        z, y, x = row // (side * side), (row // side) % side, row % side
        parent = ((z // 2) * half + y // 2) * half + x // 2 + first
        pulled = dot(ones_where(col == parent), coeffs).astype(BF)
        r = iota((rows, 128), 0) + start
        octant = 4 * ((r // (side * side)) % 2) + 2 * ((r // side) % 2) + r % 2
        total = None
        for o in range(8):
            part = dot(jnp.where(octant == o, pulled, jnp.zeros_like(pulled)), transfer_ref[o], NT)
            total = part if total is None else total + part
        return total

    top = 0.25 * far[128:144] + split_down(coeffs, 1, 2 * me, 0, 16)
    mid = 0.5 * far[0:128] + split_down(top.astype(BF), 2, 0, 0, 128)
    mid_ref[0:128, :] = mid.astype(BF)

    def leaf_chunk(c, _):
        for half in range(2):
            start = pl.multiple_of(c * 256 + half * 128, 128)
            offset = (leaf_list[:, pl.ds(start, 128)].T - c * 256 - half * 128 + 192) & 1023
            for layer in range(2):
                base = pl.multiple_of(start + layer * 64, 64)
                place = (offset[layer * 64 : (layer + 1) * 64] - 64 * layer) & 1023
                place = jnp.where(place < 128, place, place - 192)
                table = jnp.concatenate(
                    [leaf_ref[pl.ds(base, 128), :], leaf_ref[pl.ds(base + 320, 128), :]], axis=0
                )
                pick(place, 64, half * 128 + layer * 64, table)
        leaf = dot(far_pick[...], weight_ref[...], NT) + split_down(mid_ref[0:128, :], 4, 0, c * 256, 256)
        leaf = leaf.astype(BF)
        coeff_ref[rows_of(c, 256), :] = leaf
        wide = leaf.astype(F32)
        wide = wide + pltpu.roll(wide, 64, 1)
        packed = jnp.where(iota((128, 128), 1) < 64, wide[0:128], wide[128:256])
        coeff_part[rows_of(c, 128), :] = packed.astype(BF)
        for copy in to_orbs(coeff_part, coeff_other, coeff_send, coeff_recv, c, 128):
            copy.start()
        return 0

    lax.fori_loop(0, 4, leaf_chunk, 0)

    def store(c):
        rows = rows_of(c, 256)
        return pltpu.make_async_copy(orb_ref.at[:, rows], out_hbm.at[:, rows], out_sem.at[c])

    def relax_chunk(c, _):
        for copy in to_orbs(near_part, near_other, near_send, near_recv, c, 256):
            copy.wait()
        for copy in to_orbs(coeff_part, coeff_other, coeff_send, coeff_recv, c, 128):
            copy.wait()
        rows, packed_rows = rows_of(c, 256), rows_of(c, 128)
        packed = coeff_part[packed_rows, :].astype(F32)
        hartree = near_part[rows, :].astype(F32)
        for away in range(orbs - 1):
            packed = packed + coeff_other[away, packed_rows, :].astype(F32)
            hartree = hartree + near_other[away, rows, :].astype(F32)
        both = dot(packed.astype(BF), basis2_ref[...])
        hartree = hartree + jnp.concatenate([both[:, :256], both[:, 256:]], axis=0)
        potential = near_ref[rows, :] + dot(coeff_ref[rows, :], basis2_ref[...])
        for o in range(2):
            values = orb_ref[o, rows, :]
            orb_ref[o, rows, :] = values - RELAX_STEP * (hartree - potential[:, o * 256 : (o + 1) * 256]) * values
        store(c).start()
        return 0

    lax.fori_loop(0, 4, relax_chunk, 0)
    for c in range(4):
        store(c).wait()


def shards(
    orbitals, near_source, far_leaf, far_mid, far_top, leaf_basis, near_table, transfer, coupling, pair_transfer,
    coarse_coupling,
):
    count, orbs = lax.axis_size("space"), lax.axis_size("orb")
    near_by, here = pl.BlockSpec(memory_space=pl.ANY), pl.BlockSpec(memory_space=pltpu.VMEM)
    return pl.pallas_call(
        step_kernel,
        in_specs=[near_by, here, here, here, here, here, near_by, here, near_by, here, here],
        out_specs=near_by,
        out_shape=jax.ShapeDtypeStruct((2, 1024, 256), F32),
        scratch_shapes=[
            pltpu.VMEM((2, 1024, 256), F32),
            pltpu.VMEM((27, 256, 256), BF),
            pltpu.VMEM((108, 64, 64), BF),
            pltpu.VMEM((1152, 512), BF),
            pltpu.VMEM((1408, 128), BF),
            pltpu.VMEM((256, 128), BF),
            pltpu.VMEM((128, 128), BF),
            pltpu.VMEM((count * 16, 128), BF),
            pltpu.VMEM((128, 512), BF),
            pltpu.VMEM((8, 128, 128), BF),
            pltpu.VMEM((2, 128, 128), BF),
            pltpu.VMEM((4, 128, 128), BF),
            pltpu.VMEM((128, 108 * 128), BF),
            pltpu.VMEM((108 * 64, 256), BF),
            pltpu.VMEM((512, 27 * 256), BF),
            pltpu.VMEM((256, 108 * 128), BF),
            pltpu.VMEM((1024, 512), F32),
            pltpu.VMEM((1024, 256), BF),
            pltpu.VMEM((orbs - 1, 1024, 256), BF),
            pltpu.VMEM((1024, 128), BF),
            pltpu.VMEM((512, 128), BF),
            pltpu.VMEM((orbs - 1, 512, 128), BF),
            pltpu.SemaphoreType.DMA((6,)),
            pltpu.SemaphoreType.DMA((4,)),
            pltpu.SemaphoreType.DMA((8,)),
            pltpu.SemaphoreType.DMA((8,)),
            pltpu.SemaphoreType.DMA((count,)),
            pltpu.SemaphoreType.DMA((count,)),
            pltpu.SemaphoreType.DMA((orbs - 1, 4)),
            pltpu.SemaphoreType.DMA((orbs - 1, 4)),
            pltpu.SemaphoreType.DMA((orbs - 1, 4)),
            pltpu.SemaphoreType.DMA((orbs - 1, 4)),
        ],
        compiler_params=pltpu.CompilerParams(vmem_limit_bytes=52 << 20, collective_id=0, has_side_effects=True),
        cost_estimate=pl.CostEstimate(flops=36_000_000_000, bytes_accessed=12 << 20, transcendentals=0),
        name="step",
    )(
        orbitals, near_source.T, far_leaf.T, far_mid.T, far_top.T, leaf_basis, near_table, transfer, coupling,
        pair_transfer, coarse_coupling,
    )


def solution(mesh):
    placed = (P("orb", "space", None),) + (P("space", None),) * 4 + (P(),) * 6
    return jax.shard_map(
        shards, mesh=mesh, in_specs=placed, out_specs=P("orb", "space", None), check_vma=False
    )
```

time: 198 us -> 102 us (0.52)
  waiting for transfers between devices: 44.8 us -> 0 us
  blocking collectives: 30.3 us -> 0 us
  between operations: 13.5 us -> 0.07 us
  Pallas kernels: 83.6 us -> 93.2 us
  starting transfers between devices: 8.98 us -> 0 us
  local copies, waits for them, and re-layouts: 14.3 us -> 8.39 us
    psum x2 -> x0, waiting for transfers between devices: 44.7 us -> none  [the longest x1 44.7 us: shards(): coeff_sum = lax.psum(coeff_part, 'orb')]
    all_gather x1 -> x0, blocking collectives: 30.3 us -> none  [shards(): cubes = lax.all_gather(cube[0:2], 'space', axis=0, tiled=True)]
    pallas_call x5 -> x1, Pallas kernels: 83.6 us -> 93.2 us  [shards(): pl.pallas_call(step_kernel, in_specs=[near_by, here, here, here, here, he...]
    ppermute x4 -> x0, starting transfers between devices: 8.93 us -> none  [the longest x1 4.93 us: shards(): dens_prev = lax.ppermute(density[960:1024], 'space', to_next)]
    slice x4 -> x0, local copies, waits for them, and re-layouts: 2.91 us -> none  [the longest x3 2.03 us: shards(): transfer2, pair2, coarse2 = (small[0:8], small[8:10], small[10:14])]
    unnamed x23 -> x17, local copies, waits for them, and re-layouts: 10.6 us -> 8.39 us
  transfers between devices with their start and end apart: 6 -> 0, of which waited for: 1 -> 0; matrix products, arithmetic and copies ran while one was open for 5% -> 0% of each run, Pallas kernels for 37% -> 0%
where the time goes in v3:
time: 102 us
  Pallas kernels  93.2 us (91%)
  local copies, waits for them, and re-layouts  8.39 us (8%)
    pallas_call x1, Pallas kernels, shards(): pl.pallas_call(step_kernel, in_specs=[near_by, here, here, here, here, he...  93.2 us
    unnamed x17, local copies, waits for them, and re-layouts  8.39 us

profile of v3, /device:TPU:0, one launch (start us, length us, event | category | flops | bytes accessed | tf_op | source)
XLA Modules:
  0.0 101.7 jit_solution(12602178416682854471)
XLA Ops:
  0.0 0.0 copy-start.3
  0.0 0.0 copy-start.6
  0.0 0.0 copy-start.2
  0.0 0.0 copy-start.5
  0.0 0.0 copy-start.4
  0.0 0.0 copy-start
  0.0 0.0 copy-start.1
  0.0 0.9 copy.12
  0.9 4.4 %copy.13.coupling_hbm = bf16[108,64,64]{2,1,0:T(8,128)(2,1)} copy(bf16[108,64,64]{0,2,1:T(8,128)(2,1)} %param.19) | data formatting | bytes 1769472 | tf_op args[8]
  5.3 0.0 copy-done.3
  5.4 0.0 copy-done.6
  5.4 0.0 copy-done.2
  5.4 0.0 copy-done.5
  5.4 0.0 copy-done.4
  5.4 0.0 copy-done
  5.4 0.0 copy-done.1
  5.4 93.2 %step.1 = f32[2,1024,256]{2,1,0:T(8,128)} custom-call(f32[2,1024,256]{2,1,0:T(8,128)} %orb_hbm.1, s32[27,1024]{1,0:T(8,128)S(1)} %bitcast.6, s32[108,1024]{1,0:T(8,128)S(1)} %bitcast.5, s32[108,128]{1,0:T(8,128)S(1)} %bitcast.7, s32[108,16]{1,0:T(8,128)S(1)} %bitcast.4, bf16[64,256]{1,0:T(8,128)(2,1)S(1)} %copy-done.5, bf16[27,256,256]{2,1,0:T(8,128)(2,1)} %table_hbm.1, ...), custom_call_target="tpu_custom_call" | custom-call | flops 35999997952 | bytes 12582912 | tf_op jit(solution)/shard_map/step/pallas_call | solution.py:359
  98.6 3.0 %copy.15 = f32[2,1024,256]{2,1,0:T(8,128)} copy(f32[2,1024,256]{2,1,0:T(8,128)} %step.1) | data formatting | bytes 4194304
Async XLA Ops:
  0.0 5.4 %copy-start.3 = (bf16[4,64,64]{2,1,0:T(8,128)(2,1)S(1)}, bf16[4,64,64]{2,1,0:T(8,128)(2,1)}, u32[]{:S(2)}) copy-start(bf16[4,64,64]{2,1,0:T(8,128)(2,1)} %coarse_in.1) | copy-start | bytes 98308
  0.0 5.4 %copy-start.6 = (bf16[2,64,64]{2,1,0:T(8,128)(2,1)S(1)}, bf16[2,64,64]{2,1,0:T(8,128)(2,1)}, u32[]{:S(2)}) copy-start(bf16[2,64,64]{2,1,0:T(8,128)(2,1)} %pair_in.1) | copy-start | bytes 49156
  0.0 5.4 %copy-start.2 = (bf16[8,64,64]{2,1,0:T(8,128)(2,1)S(1)}, bf16[8,64,64]{2,1,0:T(8,128)(2,1)}, u32[]{:S(2)}) copy-start(bf16[8,64,64]{2,1,0:T(8,128)(2,1)} %transfer_in.1) | copy-start | bytes 196612
  0.0 5.4 %copy-start.5 = (bf16[64,256]{1,0:T(8,128)(2,1)S(1)}, bf16[64,256]{1,0:T(8,128)(2,1)}, u32[]{:S(2)}) copy-start(bf16[64,256]{1,0:T(8,128)(2,1)} %basis_ref.1) | copy-start | bytes 98308
  0.0 5.4 %copy-start.4 = (s32[128,108]{0,1:T(8,128)S(1)}, s32[128,108]{0,1:T(8,128)}, u32[]{:S(2)}) copy-start(s32[128,108]{0,1:T(8,128)} %param.14) | copy-start | bytes 165892
  0.0 5.4 %copy-start = (s32[1024,108]{0,1:T(8,128)S(1)}, s32[1024,108]{0,1:T(8,128)}, u32[]{:S(2)}) copy-start(s32[1024,108]{0,1:T(8,128)} %param.13) | copy-start | bytes 1327108
  0.0 5.4 %copy-start.1 = (s32[1024,27]{0,1:T(8,128)S(1)}, s32[1024,27]{0,1:T(8,128)}, u32[]{:S(2)}) copy-start(s32[1024,27]{0,1:T(8,128)} %param.12) | copy-start | bytes 331780

commit v4 on v3

--- a/solution.py
+++ b/solution.py
@@ -25,8 +25,16 @@
     return jnp.where(mask, 1.0, 0.0).astype(BF)
 
 
-def one_hot(column, rows, width):
-    return ones_where(iota((rows, width), 1) == column)
+def one_hot(places, first, number, rows, width):
+    lane = iota((rows, width), 1).astype(BF)
+    found = [
+        jnp.where(lane == places[:, k : k + 1], BF(1), BF(0)) for k in range(first, first + number)
+    ]
+    return jnp.concatenate(found, axis=0)
+
+
+def as_place(numbers):
+    return numbers.astype(F32).astype(BF)
 
 
 def octant_picker(parents, half, width):
@@ -61,10 +69,10 @@
 
 def step_kernel(
     orb_hbm, near_list, leaf_list, mid_list, top_list, basis_ref, table_hbm, transfer_in, coupling_hbm, pair_in, coarse_in,
-    out_hbm,
+    out_ref,
     orb_ref, table_ref, coupling_ref, dens_ref, leaf_ref, mid_ref, top_ref, cube_ref, basis2_ref, transfer_ref, pair_ref,
-    coarse_ref, weight_ref, hot_ref, near_pick, far_pick, near_ref, near_part, near_other, coeff_ref, coeff_part, coeff_other,
-    load_sem, out_sem, halo_send, halo_recv, cube_send, cube_recv, near_send, near_recv, coeff_send, coeff_recv,
+    coarse_ref, weight_ref, near_pick, far_pick, near_ref, near_part, near_other, coeff_ref, coeff_part, coeff_other,
+    load_sem, halo_send, halo_recv, cube_send, cube_recv, near_send, near_recv, coeff_send, coeff_recv,
 ):
     me, orb = lax.axis_index("space"), lax.axis_index("orb")
     count, orbs = lax.axis_size("space"), lax.axis_size("orb")
@@ -191,15 +199,14 @@
 
         for part in range(2):
             base = pl.multiple_of(c * 256 + part * 128, 128)
-            place = (near_list[:, pl.ds(base, 128)].T + (64 + 128 * part)) & 255
-            for k in range(27):
-                hot_ref[k * 128 : (k + 1) * 128, :] = one_hot(place[:, k : k + 1], 128, 256)
-            for o in range(2):
-                source = dens_ref[pl.ds(base, 256), o * 256 : (o + 1) * 256]
-                at = o * 256 + part * 128
-                for first in range(0, 27, 9):
-                    picked = dot(hot_ref[first * 128 : (first + 9) * 128, :], source).astype(BF)
-                    for k in range(9):
+            place = as_place((near_list[:, pl.ds(base, 128)].T + (64 + 128 * part)) & 255)
+            for first in range(0, 27, 3):
+                hot = one_hot(place, first, 3, 128, 256)
+                for o in range(2):
+                    source = dens_ref[pl.ds(base, 256), o * 256 : (o + 1) * 256]
+                    at = o * 256 + part * 128
+                    picked = dot(hot, source).astype(BF)
+                    for k in range(3):
                         near_pick[at : at + 128, (first + k) * 256 : (first + k + 1) * 256] = picked[
                             k * 128 : (k + 1) * 128
                         ]
@@ -224,12 +231,13 @@
         copy.wait()
 
     def pick(place, rows, at, table):
-        width = table.shape[0]
-        for k in range(108):
-            hot_ref[k * rows : (k + 1) * rows, :width] = one_hot(place[:, k : k + 1], rows, width)
-        for first in range(0, 108, 12):
-            picked = dot(hot_ref[first * rows : (first + 12) * rows, :width], table).astype(BF)
-            for k in range(12):
+        number = 128 // rows
+        place = as_place(place)
+        for first in range(0, 108, number):
+            number = min(number, 108 - first)
+            hot = one_hot(place, first, number, rows, table.shape[0])
+            picked = dot(hot, table).astype(BF)
+            for k in range(number):
                 far_pick[at : at + rows, (first + k) * 128 : (first + k + 1) * 128] = picked[
                     k * rows : (k + 1) * rows
                 ]
@@ -321,11 +329,7 @@
 
     lax.fori_loop(0, 4, leaf_chunk, 0)
 
-    def store(c):
-        rows = rows_of(c, 256)
-        return pltpu.make_async_copy(orb_ref.at[:, rows], out_hbm.at[:, rows], out_sem.at[c])
-
-    def relax_chunk(c, _):
+    def change_chunk(c, _):
         for copy in to_orbs(near_part, near_other, near_send, near_recv, c, 256):
             copy.wait()
         for copy in to_orbs(coeff_part, coeff_other, coeff_send, coeff_recv, c, 128):
@@ -340,14 +344,10 @@
         hartree = hartree + jnp.concatenate([both[:, :256], both[:, 256:]], axis=0)
         potential = near_ref[rows, :] + dot(coeff_ref[rows, :], basis2_ref[...])
         for o in range(2):
-            values = orb_ref[o, rows, :]
-            orb_ref[o, rows, :] = values - RELAX_STEP * (hartree - potential[:, o * 256 : (o + 1) * 256]) * values
-        store(c).start()
-        return 0
-
-    lax.fori_loop(0, 4, relax_chunk, 0)
-    for c in range(4):
-        store(c).wait()
+            out_ref[o, rows, :] = hartree - potential[:, o * 256 : (o + 1) * 256]
+        return 0
+
+    lax.fori_loop(0, 4, change_chunk, 0)
 
 
 def shards(
@@ -356,10 +356,10 @@
 ):
     count, orbs = lax.axis_size("space"), lax.axis_size("orb")
     near_by, here = pl.BlockSpec(memory_space=pl.ANY), pl.BlockSpec(memory_space=pltpu.VMEM)
-    return pl.pallas_call(
+    change = pl.pallas_call(
         step_kernel,
         in_specs=[near_by, here, here, here, here, here, near_by, here, near_by, here, here],
-        out_specs=near_by,
+        out_specs=here,
         out_shape=jax.ShapeDtypeStruct((2, 1024, 256), F32),
         scratch_shapes=[
             pltpu.VMEM((2, 1024, 256), F32),
@@ -375,7 +375,6 @@
             pltpu.VMEM((2, 128, 128), BF),
             pltpu.VMEM((4, 128, 128), BF),
             pltpu.VMEM((128, 108 * 128), BF),
-            pltpu.VMEM((108 * 64, 256), BF),
             pltpu.VMEM((512, 27 * 256), BF),
             pltpu.VMEM((256, 108 * 128), BF),
             pltpu.VMEM((1024, 512), F32),
@@ -385,7 +384,6 @@
             pltpu.VMEM((512, 128), BF),
             pltpu.VMEM((orbs - 1, 512, 128), BF),
             pltpu.SemaphoreType.DMA((6,)),
-            pltpu.SemaphoreType.DMA((4,)),
             pltpu.SemaphoreType.DMA((8,)),
             pltpu.SemaphoreType.DMA((8,)),
             pltpu.SemaphoreType.DMA((count,)),
@@ -395,13 +393,14 @@
             pltpu.SemaphoreType.DMA((orbs - 1, 4)),
             pltpu.SemaphoreType.DMA((orbs - 1, 4)),
         ],
-        compiler_params=pltpu.CompilerParams(vmem_limit_bytes=52 << 20, collective_id=0, has_side_effects=True),
+        compiler_params=pltpu.CompilerParams(vmem_limit_bytes=48 << 20, collective_id=0, has_side_effects=True),
         cost_estimate=pl.CostEstimate(flops=36_000_000_000, bytes_accessed=12 << 20, transcendentals=0),
         name="step",
     )(
         orbitals, near_source.T, far_leaf.T, far_mid.T, far_top.T, leaf_basis, near_table, transfer, coupling,
         pair_transfer, coarse_coupling,
     )
+    return orbitals - RELAX_STEP * change * orbitals
 
 
 def solution(mesh):

time: 102 us -> 77.2 us (0.76)
  Pallas kernels: 93.2 us -> 70.4 us
  local copies, waits for them, and re-layouts: 8.39 us -> 4.66 us
  other arithmetic: 0 us -> 1.59 us
    pallas_call x1, Pallas kernels: 93.2 us -> 70.4 us  [shards(): pl.pallas_call(step_kernel, in_specs=[near_by, here, here, here, here, he...]
    unnamed x17 -> x18, local copies, waits for them, and re-layouts: 8.39 us -> 4.66 us
    sub x0 -> x1, other arithmetic: none -> 1.59 us  [shards(): return orbitals - RELAX_STEP * change * orbitals]
where the time goes in v4:
time: 77.2 us; the launch traced here: 76.8 us
  Pallas kernels  70.4 us (91%)
  local copies, waits for them, and re-layouts  4.66 us (6%)
  other arithmetic  1.59 us (2%)
    pallas_call x1, Pallas kernels, shards(): pl.pallas_call(step_kernel, in_specs=[near_by, here, here, here, here, he...  70.4 us
    unnamed x18, local copies, waits for them, and re-layouts  4.66 us
    sub x1, other arithmetic, shards(): return orbitals - RELAX_STEP * change * orbitals  1.59 us

profile of v4, /device:TPU:0, one launch (start us, length us, event | category | flops | bytes accessed | tf_op | source)
XLA Modules:
  0.0 76.8 jit_solution(14871741360975081349)
XLA Ops:
  0.0 0.0 copy-start.3
  0.0 0.0 copy-start.6
  0.0 0.0 copy-start.2
  0.0 0.0 copy-start.5
  0.0 0.0 copy-start.4
  0.0 0.0 copy-start
  0.0 0.0 copy-start.1
  0.0 0.9 %copy.12 = s32[16,108]{0,1:T(8,128)S(1)} copy(s32[16,108]{1,0:T(8,128)} %param.15) | data formatting | bytes 13824 | tf_op args[4]
  0.9 3.8 %copy.13.coupling_hbm = bf16[108,64,64]{2,1,0:T(8,128)(2,1)S(1)} copy(bf16[108,64,64]{0,2,1:T(8,128)(2,1)} %param.19) | data formatting | bytes 1769472 | tf_op args[8]
  4.7 0.0 copy-done.3
  4.7 0.0 copy-done.6
  4.7 0.0 copy-done.2
  4.7 0.0 copy-done.5
  4.7 0.0 copy-done.4
  4.7 0.0 copy-done
  4.7 0.0 copy-done.1
  4.7 0.0 copy-start.7
  4.8 70.4 %step.1 = f32[2,1024,256]{2,1,0:T(8,128)S(1)} custom-call(f32[2,1024,256]{2,1,0:T(8,128)} %orb_hbm.1, s32[27,1024]{1,0:T(8,128)S(1)} %bitcast.6, s32[108,1024]{1,0:T(8,128)S(1)} %bitcast.5, s32[108,128]{1,0:T(8,128)S(1)} %bitcast.7, s32[108,16]{1,0:T(8,128)S(1)} %bitcast.4, bf16[64,256]{1,0:T(8,128)(2,1)S(1)} %copy-done.5, bf16[27,256,256]{2,1,0:T(8,128)(2,1)} %table_hbm.1, ...), custom_call_target="tpu_custom_call" | custom-call | flops 35999997952 | bytes 12582912 | tf_op jit(solution)/shard_map/step/pallas_call | solution.py:359
  75.2 0.0 copy-done.7
  75.2 1.6 %multiply_subtract_fusion = f32[2,1024,256]{2,1,0:T(8,128)} fusion(f32[2,1024,256]{2,1,0:T(8,128)S(1)} %copy-done.7, f32[2,1024,256]{2,1,0:T(8,128)S(1)} %step.1), kind=kLoop, calls=%fused_computation | loop fusion | flops 1572864 | bytes 6291456 | tf_op jit(solution)/shard_map/sub | solution.py:403
Async XLA Ops:
  0.0 4.7 %copy-start.3 = (bf16[4,64,64]{2,1,0:T(8,128)(2,1)S(1)}, bf16[4,64,64]{2,1,0:T(8,128)(2,1)}, u32[]{:S(2)}) copy-start(bf16[4,64,64]{2,1,0:T(8,128)(2,1)} %coarse_in.1) | copy-start | bytes 98308
  0.0 4.7 %copy-start.6 = (bf16[2,64,64]{2,1,0:T(8,128)(2,1)S(1)}, bf16[2,64,64]{2,1,0:T(8,128)(2,1)}, u32[]{:S(2)}) copy-start(bf16[2,64,64]{2,1,0:T(8,128)(2,1)} %pair_in.1) | copy-start | bytes 49156
  0.0 4.7 %copy-start.2 = (bf16[8,64,64]{2,1,0:T(8,128)(2,1)S(1)}, bf16[8,64,64]{2,1,0:T(8,128)(2,1)}, u32[]{:S(2)}) copy-start(bf16[8,64,64]{2,1,0:T(8,128)(2,1)} %transfer_in.1) | copy-start | bytes 196612
  0.0 4.7 %copy-start.5 = (bf16[64,256]{1,0:T(8,128)(2,1)S(1)}, bf16[64,256]{1,0:T(8,128)(2,1)}, u32[]{:S(2)}) copy-start(bf16[64,256]{1,0:T(8,128)(2,1)} %basis_ref.1) | copy-start | bytes 98308
  0.0 4.7 %copy-start.4 = (s32[128,108]{0,1:T(8,128)S(1)}, s32[128,108]{0,1:T(8,128)}, u32[]{:S(2)}) copy-start(s32[128,108]{0,1:T(8,128)} %param.14) | copy-start | bytes 165892
  0.0 4.7 %copy-start = (s32[1024,108]{0,1:T(8,128)S(1)}, s32[1024,108]{0,1:T(8,128)}, u32[]{:S(2)}) copy-start(s32[1024,108]{0,1:T(8,128)} %param.13) | copy-start | bytes 1327108
  0.0 4.7 %copy-start.1 = (s32[1024,27]{0,1:T(8,128)S(1)}, s32[1024,27]{0,1:T(8,128)}, u32[]{:S(2)}) copy-start(s32[1024,27]{0,1:T(8,128)} %param.12) | copy-start | bytes 331780
  4.7 70.5 %copy-start.7 = (f32[2,1024,256]{2,1,0:T(8,128)S(1)}, f32[2,1024,256]{2,1,0:T(8,128)}, u32[]{:S(2)}) copy-start(f32[2,1024,256]{2,1,0:T(8,128)} %orb_hbm.1) | copy-start | bytes 6291460

commit v5 on v4

--- a/solution.py
+++ b/solution.py
@@ -70,7 +70,7 @@
 def step_kernel(
     orb_hbm, near_list, leaf_list, mid_list, top_list, basis_ref, table_hbm, transfer_in, coupling_hbm, pair_in, coarse_in,
     out_ref,
-    orb_ref, table_ref, coupling_ref, dens_ref, leaf_ref, mid_ref, top_ref, cube_ref, basis2_ref, transfer_ref, pair_ref,
+    orb_ref, table_ref, coupling_ref, turned_ref, dens_ref, leaf_ref, mid_ref, top_ref, cube_ref, basis2_ref, transfer_ref, pair_ref,
     coarse_ref, weight_ref, near_pick, far_pick, near_ref, near_part, near_other, coeff_ref, coeff_part, coeff_other,
     load_sem, halo_send, halo_recv, cube_send, cube_recv, near_send, near_recv, coeff_send, coeff_recv,
 ):
@@ -79,15 +79,14 @@
     after, before = lax.rem(me + 1, count), lax.rem(me + count - 1, count)
     barrier = pltpu.get_barrier_semaphore()
 
-    def greet(i, _):
-        other = lax.rem(me + i, count)
-        pl.semaphore_signal(barrier, inc=1, device_id=(other, orb), device_id_type=MESH)
-        return 0
-
-    lax.fori_loop(1, count, greet, 0)
-    for away in range(1, orbs):
-        other = lax.rem(orb + away, orbs)
-        pl.semaphore_signal(barrier, inc=1, device_id=(me, other), device_id_type=MESH)
+    group = min(8, count)
+    base = me - lax.rem(me, group)
+    mates = [base + lax.rem(me - base + away, group) for away in range(1, group)]
+    twins = [lax.rem(me + away, count) for away in range(group, count, group)]
+    friends = [(other, orb) for other in mates + twins + [before, after]]
+    friends += [(me, lax.rem(orb + away, orbs)) for away in range(1, orbs)]
+    for friend in friends:
+        pl.semaphore_signal(barrier, inc=1, device_id=friend, device_id_type=MESH)
 
     def rows_of(c, size):
         return pl.ds(pl.multiple_of(c * size, size), size)
@@ -124,7 +123,6 @@
         return 0
 
     lax.fori_loop(0, 4, moments_chunk, 0)
-    pl.semaphore_wait(barrier, count - 1 + orbs - 1)
 
     def halo(number, ref, head, tail, rows, ahead):
         source, target, device = (tail, 0, after) if ahead else (head, tail + rows, before)
@@ -146,32 +144,28 @@
     ):
         for ahead in (False, True):
             halos.append(halo(len(halos), ref, head, tail, rows, ahead))
-    for copy in halos[0:6]:
-        copy.start()
     top = merge_up(dot(octant_picker(16, 2, 128), mid_ref[48:176, :]).astype(BF), 16, transfer_ref)
     top_ref[16:32, :] = top
-    for copy in halos[6:8]:
-        copy.start()
     cube_ref[rows_of(me, 16), :] = merge_up(
         dot(octant_picker(16, 1, 16), top).astype(BF), 16, transfer_ref
     )
 
-    def cube_copy(other, owner):
-        block = cube_ref.at[rows_of(owner, 16)]
-        return pltpu.make_async_remote_copy(
-            src_ref=block,
-            dst_ref=block,
-            send_sem=cube_send.at[other],
-            recv_sem=cube_recv.at[owner],
-            device_id=(other, orb),
-            device_id_type=MESH,
-        )
-
-    def send_cube(i, _):
-        cube_copy(lax.rem(me + i, count), me).start()
-        return 0
-
-    lax.fori_loop(1, count, send_cube, 0)
+    def cube_copies(first, blocks, others, stage):
+        block = cube_ref.at[pl.ds(pl.multiple_of(first * 16, 16), blocks * 16)]
+        return [
+            pltpu.make_async_remote_copy(
+                src_ref=block,
+                dst_ref=block,
+                send_sem=cube_send.at[stage + i],
+                recv_sem=cube_recv.at[stage + i],
+                device_id=(other, orb),
+                device_id_type=MESH,
+            )
+            for i, other in enumerate(others)
+        ]
+
+    to_mates = cube_copies(me, 1, mates, 0)
+    to_twins = cube_copies(base, group, twins, group - 1)
 
     def to_orbs(part, landing, send, recv, c, size):
         rows = rows_of(c, size)
@@ -188,14 +182,31 @@
         ]
 
     load_table.wait()
+    load_coupling.wait()
 
     def near_chunk(i, _):
         c = lax.rem(i + 1, 4)
 
+        @pl.when(i == 1)
+        def _():
+            pl.semaphore_wait(barrier, len(friends))
+            for copy in halos + to_mates:
+                copy.start()
+
+        @pl.when(i >= 1)
+        def _():
+            for copy in to_orbs(near_part, near_other, near_send, near_recv, i, 256):
+                copy.start()
+
         @pl.when(i == 2)
         def _():
-            for copy in halos[0:2]:
+            for copy in halos[0:2] + to_mates:
                 copy.wait()
+            for copy in to_twins:
+                copy.start()
+
+        for r in range(16):
+            turned_ref[i * 16 + r] = coupling_ref[i * 16 + r].astype(F32).T
 
         for part in range(2):
             base = pl.multiple_of(c * 256 + part * 128, 128)
@@ -218,15 +229,14 @@
         near_ref[rows, 0:256] = total[:256]
         near_ref[rows, 256:512] = total[256:]
         near_part[rows, :] = (total[:256] + total[256:]).astype(BF)
-        for copy in to_orbs(near_part, near_other, near_send, near_recv, c, 256):
-            copy.start()
         return 0
 
     lax.fori_loop(0, 4, near_chunk, 0)
-
-    load_coupling.wait()
+    for copy in to_orbs(near_part, near_other, near_send, near_recv, 0, 256):
+        copy.start()
+
     for k in range(108):
-        weight_ref[:, k * 128 : (k + 1) * 128] = spread(coupling_ref[k])
+        weight_ref[:, k * 128 : (k + 1) * 128] = spread(turned_ref[:, k, :].astype(BF))
     for copy in halos[2:8]:
         copy.wait()
 
@@ -245,16 +255,11 @@
     mid_place = mid_list[...].T - (me * 128 - 48)
     pick(mid_place[0:64], 64, 0, mid_ref[...])
     pick(mid_place[64:128], 64, 64, mid_ref[...])
-    pick(top_list[...].T - (me * 16 - 16), 16, 128, top_ref[...])
+    pick(top_list[...] - (me * 16 - 16), 16, 128, top_ref[...])
     far = dot(far_pick[0:144, :], weight_ref[...], NT)
 
-    def wait_cube(i, _):
-        other = lax.rem(me + i, count)
-        cube_copy(other, me).wait_send()
-        cube_copy(other, other).wait_recv()
-        return 0
-
-    lax.fori_loop(1, count, wait_cube, 0)
+    for copy in to_twins:
+        copy.wait()
     row, col = iota((64, cube_ref.shape[0]), 0), iota((64, cube_ref.shape[0]), 1)
     cubes = dot(ones_where(col == 16 * (row // 2) + row % 2), cube_ref[...]).astype(BF)
     row, col = iota((64, 64), 0), iota((64, 64), 1)
@@ -364,7 +369,8 @@
         scratch_shapes=[
             pltpu.VMEM((2, 1024, 256), F32),
             pltpu.VMEM((27, 256, 256), BF),
-            pltpu.VMEM((108, 64, 64), BF),
+            pltpu.VMEM((64, 64, 108), BF),
+            pltpu.VMEM((64, 108, 64), F32),
             pltpu.VMEM((1152, 512), BF),
             pltpu.VMEM((1408, 128), BF),
             pltpu.VMEM((256, 128), BF),
@@ -386,8 +392,8 @@
             pltpu.SemaphoreType.DMA((6,)),
             pltpu.SemaphoreType.DMA((8,)),
             pltpu.SemaphoreType.DMA((8,)),
-            pltpu.SemaphoreType.DMA((count,)),
-            pltpu.SemaphoreType.DMA((count,)),
+            pltpu.SemaphoreType.DMA((16,)),
+            pltpu.SemaphoreType.DMA((16,)),
             pltpu.SemaphoreType.DMA((orbs - 1, 4)),
             pltpu.SemaphoreType.DMA((orbs - 1, 4)),
             pltpu.SemaphoreType.DMA((orbs - 1, 4)),
@@ -397,8 +403,8 @@
         cost_estimate=pl.CostEstimate(flops=36_000_000_000, bytes_accessed=12 << 20, transcendentals=0),
         name="step",
     )(
-        orbitals, near_source.T, far_leaf.T, far_mid.T, far_top.T, leaf_basis, near_table, transfer, coupling,
-        pair_transfer, coarse_coupling,
+        orbitals, near_source.T, far_leaf.T, far_mid.T, far_top, leaf_basis, near_table, transfer,
+        jnp.transpose(coupling, (1, 2, 0)), pair_transfer, coarse_coupling,
     )
     return orbitals - RELAX_STEP * change * orbitals
 

time: 77.2 us -> 84.5 us (1.095)
  local copies, waits for them, and re-layouts: 4.66 us -> 9.51 us
  Pallas kernels: 70.4 us -> 72.8 us
    unnamed x18 -> x20, local copies, waits for them, and re-layouts: 4.66 us -> 9.51 us
    pallas_call x1, Pallas kernels: 70.4 us -> 72.8 us  [shards(): pl.pallas_call(step_kernel, in_specs=[near_by, here, here, here, here, he...]
where the time goes in v5:
time: 84.5 us; the launch traced here: 84 us
  Pallas kernels  72.8 us (86%)
  local copies, waits for them, and re-layouts  9.51 us (11%)
  other arithmetic  1.59 us (2%)
    pallas_call x1, Pallas kernels, shards(): pl.pallas_call(step_kernel, in_specs=[near_by, here, here, here, here, he...  72.8 us
    unnamed x20, local copies, waits for them, and re-layouts  9.51 us

profile of v5, /device:TPU:0, one launch (start us, length us, event | category | flops | bytes accessed | tf_op | source)
XLA Modules:
  0.0 84.0 jit_solution(9393924622726475502)
XLA Ops:
  0.0 0.0 copy-start
  0.0 1.6 %copy-done = f32[2,1024,256]{2,1,0:T(8,128)S(1)} copy-done((f32[2,1024,256]{2,1,0:T(8,128)S(1)}, f32[2,1024,256]{2,1,0:T(8,128)}, u32[]{:S(2)}) %copy-start) | copy-done | bytes 2097176
  1.6 0.0 copy-start.1
  1.6 1.2 %copy-done.1 = bf16[108,64,64]{0,2,1:T(8,128)(2,1)S(1)} copy-done((bf16[108,64,64]{0,2,1:T(8,128)(2,1)S(1)}, bf16[108,64,64]{0,2,1:T(8,128)(2,1)}, u32[]{:S(2)}) %copy-start.1) | copy-done | bytes 884760
  2.8 0.0 copy-start.2
  2.8 1.0 %copy-done.2 = s32[1024,108]{0,1:T(8,128)S(1)} copy-done((s32[1024,108]{0,1:T(8,128)S(1)}, s32[1024,108]{0,1:T(8,128)}, u32[]{:S(2)}) %copy-start.2) | copy-done | bytes 442392
  3.8 0.0 copy-start.3
  3.8 0.9 %copy-done.3 = s32[1024,27]{0,1:T(8,128)S(1)} copy-done((s32[1024,27]{0,1:T(8,128)S(1)}, s32[1024,27]{0,1:T(8,128)}, u32[]{:S(2)}) %copy-start.3) | copy-done | bytes 110616
  4.7 0.0 copy-start.4
  4.7 0.9 %copy-done.4 = bf16[8,64,64]{2,1,0:T(8,128)(2,1)S(1)} copy-done((bf16[8,64,64]{2,1,0:T(8,128)(2,1)S(1)}, bf16[8,64,64]{2,1,0:T(8,128)(2,1)}, u32[]{:S(2)}) %copy-start.4) | copy-done | bytes 65560
  5.6 0.0 copy-start.5
  5.6 0.8 copy-done.5
  6.5 0.0 copy-start.6
  6.5 0.8 copy-done.6
  7.3 0.0 copy-start.7
  7.3 0.8 copy-done.7
  8.1 0.0 copy-start.8
  8.1 0.8 copy-done.8
  8.8 0.0 copy-start.9
  8.8 0.7 copy-done.9
  9.5 72.8 %step.1 = f32[2,1024,256]{2,1,0:T(8,128)S(1)} custom-call(f32[2,1024,256]{2,1,0:T(8,128)S(1)} %copy-done, s32[27,1024]{1,0:T(8,128)S(1)} %bitcast.6, s32[108,1024]{1,0:T(8,128)S(1)} %bitcast.5, s32[108,128]{1,0:T(8,128)S(1)} %bitcast.7, s32[16,108]{1,0:T(8,128)S(1)} %copy-done.9, bf16[64,256]{1,0:T(8,128)(2,1)S(1)} %copy-done.7, ...), custom_call_target="tpu_custom_call" | custom-call | flops 35999997952 | bytes 12582912 | tf_op jit(solution)/shard_map/step/pallas_call | solution.py:364
  82.4 1.6 %multiply_subtract_fusion = f32[2,1024,256]{2,1,0:T(8,128)} fusion(f32[2,1024,256]{2,1,0:T(8,128)S(1)} %copy-done, f32[2,1024,256]{2,1,0:T(8,128)S(1)} %step.1), kind=kLoop, calls=%fused_computation | loop fusion | flops 1572864 | bytes 6291456 | tf_op jit(solution)/shard_map/sub | solution.py:409
Async XLA Ops:
  0.0 1.6 %copy-start = (f32[2,1024,256]{2,1,0:T(8,128)S(1)}, f32[2,1024,256]{2,1,0:T(8,128)}, u32[]{:S(2)}) copy-start(f32[2,1024,256]{2,1,0:T(8,128)} %orb_hbm.1) | copy-start | bytes 6291460
  1.6 1.2 %copy-start.1 = (bf16[108,64,64]{0,2,1:T(8,128)(2,1)S(1)}, bf16[108,64,64]{0,2,1:T(8,128)(2,1)}, u32[]{:S(2)}) copy-start(bf16[108,64,64]{0,2,1:T(8,128)(2,1)} %param.19) | copy-start | bytes 2654212
  2.8 1.0 %copy-start.2 = (s32[1024,108]{0,1:T(8,128)S(1)}, s32[1024,108]{0,1:T(8,128)}, u32[]{:S(2)}) copy-start(s32[1024,108]{0,1:T(8,128)} %param.13) | copy-start | bytes 1327108
  3.8 0.9 %copy-start.3 = (s32[1024,27]{0,1:T(8,128)S(1)}, s32[1024,27]{0,1:T(8,128)}, u32[]{:S(2)}) copy-start(s32[1024,27]{0,1:T(8,128)} %param.12) | copy-start | bytes 331780
  4.7 0.9 %copy-start.4 = (bf16[8,64,64]{2,1,0:T(8,128)(2,1)S(1)}, bf16[8,64,64]{2,1,0:T(8,128)(2,1)}, u32[]{:S(2)}) copy-start(bf16[8,64,64]{2,1,0:T(8,128)(2,1)} %transfer_in.1) | copy-start | bytes 196612
  5.6 0.8 copy-start.5
  6.5 0.8 copy-start.6
  7.3 0.8 copy-start.7
  8.1 0.8 copy-start.8
  8.8 0.7 copy-start.9

commit v6 on v5

--- a/solution.py
+++ b/solution.py
@@ -70,8 +70,8 @@
 def step_kernel(
     orb_hbm, near_list, leaf_list, mid_list, top_list, basis_ref, table_hbm, transfer_in, coupling_hbm, pair_in, coarse_in,
     out_ref,
-    orb_ref, table_ref, coupling_ref, turned_ref, dens_ref, leaf_ref, mid_ref, top_ref, cube_ref, basis2_ref, transfer_ref, pair_ref,
-    coarse_ref, weight_ref, near_pick, far_pick, near_ref, near_part, near_other, coeff_ref, coeff_part, coeff_other,
+    orb_ref, table_ref, coupling_ref, dens_ref, leaf_ref, mid_ref, top_ref, cube_ref, basis2_ref, transfer_ref, pair_ref,
+    coarse_ref, weight_ref, near_pick, far_pick, near_ref, near_part, near_other, far_ref, coeff_ref, coeff_part, coeff_other,
     load_sem, halo_send, halo_recv, cube_send, cube_recv, near_send, near_recv, coeff_send, coeff_recv,
 ):
     me, orb = lax.axis_index("space"), lax.axis_index("orb")
@@ -204,9 +204,6 @@
                 copy.wait()
             for copy in to_twins:
                 copy.start()
-
-        for r in range(16):
-            turned_ref[i * 16 + r] = coupling_ref[i * 16 + r].astype(F32).T
 
         for part in range(2):
             base = pl.multiple_of(c * 256 + part * 128, 128)
@@ -231,14 +228,9 @@
         near_part[rows, :] = (total[:256] + total[256:]).astype(BF)
         return 0
 
-    lax.fori_loop(0, 4, near_chunk, 0)
-    for copy in to_orbs(near_part, near_other, near_send, near_recv, 0, 256):
-        copy.start()
-
+    lax.fori_loop(0, 2, near_chunk, 0)
     for k in range(108):
-        weight_ref[:, k * 128 : (k + 1) * 128] = spread(turned_ref[:, k, :].astype(BF))
-    for copy in halos[2:8]:
-        copy.wait()
+        weight_ref[:, k * 128 : (k + 1) * 128] = spread(coupling_ref[k])
 
     def pick(place, rows, at, table):
         number = 128 // rows
@@ -251,6 +243,32 @@
                 far_pick[at : at + rows, (first + k) * 128 : (first + k + 1) * 128] = picked[
                     k * rows : (k + 1) * rows
                 ]
+
+    def far_chunk(c):
+        for half in range(2):
+            start = pl.multiple_of(c * 256 + half * 128, 128)
+            offset = (leaf_list[:, pl.ds(start, 128)].T - start + 192) & 1023
+            for layer in range(2):
+                base = pl.multiple_of(start + layer * 64, 64)
+                table = jnp.concatenate(
+                    [leaf_ref[pl.ds(base, 128), :], leaf_ref[pl.ds(base + 320, 128), :]], axis=0
+                )
+                place = (offset[layer * 64 : (layer + 1) * 64] - 64 * layer) & 1023
+                place = jnp.where(place < 128, place, place - 192)
+                pick(place, 64, half * 128 + layer * 64, table)
+        far_ref[rows_of(c, 256), :] = dot(far_pick[...], weight_ref[...], NT)
+
+    def inner_far(i, _):
+        far_chunk(i + 1)
+        return 0
+
+    lax.fori_loop(0, 2, inner_far, 0)
+    lax.fori_loop(2, 4, near_chunk, 0)
+    for copy in to_orbs(near_part, near_other, near_send, near_recv, 0, 256):
+        copy.start()
+
+    for copy in halos[2:8]:
+        copy.wait()
 
     mid_place = mid_list[...].T - (me * 128 - 48)
     pick(mid_place[0:64], 64, 0, mid_ref[...])
@@ -309,19 +327,8 @@
     mid = 0.5 * far[0:128] + split_down(top.astype(BF), 2, 0, 0, 128)
     mid_ref[0:128, :] = mid.astype(BF)
 
-    def leaf_chunk(c, _):
-        for half in range(2):
-            start = pl.multiple_of(c * 256 + half * 128, 128)
-            offset = (leaf_list[:, pl.ds(start, 128)].T - c * 256 - half * 128 + 192) & 1023
-            for layer in range(2):
-                base = pl.multiple_of(start + layer * 64, 64)
-                place = (offset[layer * 64 : (layer + 1) * 64] - 64 * layer) & 1023
-                place = jnp.where(place < 128, place, place - 192)
-                table = jnp.concatenate(
-                    [leaf_ref[pl.ds(base, 128), :], leaf_ref[pl.ds(base + 320, 128), :]], axis=0
-                )
-                pick(place, 64, half * 128 + layer * 64, table)
-        leaf = dot(far_pick[...], weight_ref[...], NT) + split_down(mid_ref[0:128, :], 4, 0, c * 256, 256)
+    def finish_chunk(c):
+        leaf = far_ref[rows_of(c, 256), :] + split_down(mid_ref[0:128, :], 4, 0, c * 256, 256)
         leaf = leaf.astype(BF)
         coeff_ref[rows_of(c, 256), :] = leaf
         wide = leaf.astype(F32)
@@ -330,9 +337,19 @@
         coeff_part[rows_of(c, 128), :] = packed.astype(BF)
         for copy in to_orbs(coeff_part, coeff_other, coeff_send, coeff_recv, c, 128):
             copy.start()
-        return 0
-
-    lax.fori_loop(0, 4, leaf_chunk, 0)
+
+    def finish_inner(i, _):
+        finish_chunk(i + 1)
+        return 0
+
+    def finish_outer(i, _):
+        c = lax.rem(i + 1, 4)
+        far_chunk(c)
+        finish_chunk(c)
+        return 0
+
+    lax.fori_loop(0, 2, finish_inner, 0)
+    lax.fori_loop(2, 4, finish_outer, 0)
 
     def change_chunk(c, _):
         for copy in to_orbs(near_part, near_other, near_send, near_recv, c, 256):
@@ -369,8 +386,7 @@
         scratch_shapes=[
             pltpu.VMEM((2, 1024, 256), F32),
             pltpu.VMEM((27, 256, 256), BF),
-            pltpu.VMEM((64, 64, 108), BF),
-            pltpu.VMEM((64, 108, 64), F32),
+            pltpu.VMEM((108, 64, 64), BF),
             pltpu.VMEM((1152, 512), BF),
             pltpu.VMEM((1408, 128), BF),
             pltpu.VMEM((256, 128), BF),
@@ -386,6 +402,7 @@
             pltpu.VMEM((1024, 512), F32),
             pltpu.VMEM((1024, 256), BF),
             pltpu.VMEM((orbs - 1, 1024, 256), BF),
+            pltpu.VMEM((1024, 128), F32),
             pltpu.VMEM((1024, 128), BF),
             pltpu.VMEM((512, 128), BF),
             pltpu.VMEM((orbs - 1, 512, 128), BF),
@@ -404,7 +421,7 @@
         name="step",
     )(
         orbitals, near_source.T, far_leaf.T, far_mid.T, far_top, leaf_basis, near_table, transfer,
-        jnp.transpose(coupling, (1, 2, 0)), pair_transfer, coarse_coupling,
+        coupling, pair_transfer, coarse_coupling,
     )
     return orbitals - RELAX_STEP * change * orbitals
 

time: 84.5 us -> 73.8 us (0.87)
  local copies, waits for them, and re-layouts: 9.51 us -> 3.86 us
  Pallas kernels: 72.8 us -> 68.1 us
    unnamed x20 -> x19, local copies, waits for them, and re-layouts: 9.51 us -> 3.86 us
    pallas_call x1, Pallas kernels: 72.8 us -> 68.1 us  [shards(): pl.pallas_call(step_kernel, in_specs=[near_by, here, here, here, here, he...]
where the time goes in v6:
time: 73.8 us; the launch traced here: 73.6 us
  Pallas kernels  68.1 us (92%)
  local copies, waits for them, and re-layouts  3.86 us (5%)
  other arithmetic  1.59 us (2%)
    pallas_call x1, Pallas kernels, shards(): pl.pallas_call(step_kernel, in_specs=[near_by, here, here, here, here, he...  68.1 us
    unnamed x19, local copies, waits for them, and re-layouts  3.86 us
    sub x1, other arithmetic, shards(): return orbitals - RELAX_STEP * change * orbitals  1.59 us

profile of v6, /device:TPU:0, one launch (start us, length us, event | category | flops | bytes accessed | tf_op | source)
XLA Modules:
  0.0 73.6 jit_solution(16226782328115800001)
XLA Ops:
  0.0 0.0 copy-start.3
  0.0 0.0 copy-start.6
  0.0 0.0 copy-start.2
  0.0 0.0 copy-start.5
  0.0 0.0 copy-start.7
  0.0 0.0 copy-start.4
  0.0 0.0 copy-start
  0.0 0.0 copy-start.1
  0.0 3.8 %copy.12.coupling_hbm = bf16[108,64,64]{2,1,0:T(8,128)(2,1)S(1)} copy(bf16[108,64,64]{0,2,1:T(8,128)(2,1)} %param.19) | data formatting | bytes 1769472 | tf_op args[8]
  3.9 0.0 copy-done.3
  3.9 0.0 copy-done.6
  3.9 0.0 copy-done.2
  3.9 0.0 copy-done.5
  3.9 0.0 copy-done.7
  3.9 0.0 copy-done.4
  3.9 0.0 copy-done
  3.9 0.0 copy-done.1
  4.0 0.0 copy-start.8
  4.0 68.1 %step.1 = f32[2,1024,256]{2,1,0:T(8,128)S(1)} custom-call(f32[2,1024,256]{2,1,0:T(8,128)} %orb_hbm.1, s32[27,1024]{1,0:T(8,128)S(1)} %bitcast.4, s32[108,1024]{1,0:T(8,128)S(1)} %bitcast.3, s32[108,128]{1,0:T(8,128)S(1)} %bitcast.5, s32[16,108]{1,0:T(8,128)S(1)} %copy-done.7, bf16[64,256]{1,0:T(8,128)(2,1)S(1)} %copy-done.5, ...), custom_call_target="tpu_custom_call" | custom-call | flops 35999997952 | bytes 12582912 | tf_op jit(solution)/shard_map/step/pallas_call | solution.py:381
  72.0 0.0 copy-done.8
  72.1 1.6 %multiply_subtract_fusion = f32[2,1024,256]{2,1,0:T(8,128)} fusion(f32[2,1024,256]{2,1,0:T(8,128)S(1)} %copy-done.8, f32[2,1024,256]{2,1,0:T(8,128)S(1)} %step.1), kind=kLoop, calls=%fused_computation | loop fusion | flops 1572864 | bytes 6291456 | tf_op jit(solution)/shard_map/sub | solution.py:426
Async XLA Ops:
  0.0 3.9 %copy-start.3 = (bf16[4,64,64]{2,1,0:T(8,128)(2,1)S(1)}, bf16[4,64,64]{2,1,0:T(8,128)(2,1)}, u32[]{:S(2)}) copy-start(bf16[4,64,64]{2,1,0:T(8,128)(2,1)} %coarse_in.1) | copy-start | bytes 98308
  0.0 3.9 %copy-start.6 = (bf16[2,64,64]{2,1,0:T(8,128)(2,1)S(1)}, bf16[2,64,64]{2,1,0:T(8,128)(2,1)}, u32[]{:S(2)}) copy-start(bf16[2,64,64]{2,1,0:T(8,128)(2,1)} %pair_in.1) | copy-start | bytes 49156
  0.0 3.9 %copy-start.2 = (bf16[8,64,64]{2,1,0:T(8,128)(2,1)S(1)}, bf16[8,64,64]{2,1,0:T(8,128)(2,1)}, u32[]{:S(2)}) copy-start(bf16[8,64,64]{2,1,0:T(8,128)(2,1)} %transfer_in.1) | copy-start | bytes 196612
  0.0 3.9 %copy-start.5 = (bf16[64,256]{1,0:T(8,128)(2,1)S(1)}, bf16[64,256]{1,0:T(8,128)(2,1)}, u32[]{:S(2)}) copy-start(bf16[64,256]{1,0:T(8,128)(2,1)} %basis_ref.1) | copy-start | bytes 98308
  0.0 3.9 %copy-start.7 = (s32[16,108]{1,0:T(8,128)S(1)}, s32[16,108]{1,0:T(8,128)}, u32[]{:S(2)}) copy-start(s32[16,108]{1,0:T(8,128)} %top_list.1) | copy-start | bytes 20740
  0.0 3.9 %copy-start.4 = (s32[128,108]{0,1:T(8,128)S(1)}, s32[128,108]{0,1:T(8,128)}, u32[]{:S(2)}) copy-start(s32[128,108]{0,1:T(8,128)} %param.14) | copy-start | bytes 165892
  0.0 3.9 %copy-start = (s32[1024,108]{0,1:T(8,128)S(1)}, s32[1024,108]{0,1:T(8,128)}, u32[]{:S(2)}) copy-start(s32[1024,108]{0,1:T(8,128)} %param.13) | copy-start | bytes 1327108
  0.0 3.9 %copy-start.1 = (s32[1024,27]{0,1:T(8,128)S(1)}, s32[1024,27]{0,1:T(8,128)}, u32[]{:S(2)}) copy-start(s32[1024,27]{0,1:T(8,128)} %param.12) | copy-start | bytes 331780
  4.0 68.1 %copy-start.8 = (f32[2,1024,256]{2,1,0:T(8,128)S(1)}, f32[2,1024,256]{2,1,0:T(8,128)}, u32[]{:S(2)}) copy-start(f32[2,1024,256]{2,1,0:T(8,128)} %orb_hbm.1) | copy-start | bytes 6291460

commit v7 on v6

--- a/solution.py
+++ b/solution.py
@@ -232,7 +232,7 @@
     for k in range(108):
         weight_ref[:, k * 128 : (k + 1) * 128] = spread(coupling_ref[k])
 
-    def pick(place, rows, at, table):
+    def pick(place, rows, at, table, beside=iter(())):
         number = 128 // rows
         place = as_place(place)
         for first in range(0, 108, number):
@@ -243,6 +243,7 @@
                 far_pick[at : at + rows, (first + k) * 128 : (first + k + 1) * 128] = picked[
                     k * rows : (k + 1) * rows
                 ]
+            next(beside, None)
 
     def far_chunk(c):
         for half in range(2):
@@ -270,43 +271,61 @@
     for copy in halos[2:8]:
         copy.wait()
 
+    for copy in to_twins:
+        copy.wait()
+
+    coarse_coeffs = []
+
+    def coarse_tree():
+        row, col = iota((64, cube_ref.shape[0]), 0), iota((64, cube_ref.shape[0]), 1)
+        cubes = dot(ones_where(col == 16 * (row // 2) + row % 2), cube_ref[...]).astype(BF)
+        row, col = iota((64, 64), 0), iota((64, 64), 1)
+        child = [ones_where(col == 2 * row + p) for p in range(2)]
+        mother = [ones_where((col == row // 2) & (row % 2 == p)) for p in range(2)]
+        shift = [
+            ones_where((col == row - 3) & (row % 2 == 1)),
+            ones_where(col == row - 2),
+            ones_where(col == row + 2),
+            ones_where((col == row + 3) & (row % 2 == 0)),
+        ]
+        yield
+
+        def coupled(level, depth):
+            total = None
+            for w in range(4):
+                part = dot(dot(shift[w], level).astype(BF), coarse_ref[w], NT)
+                total = part if total is None else total + part
+            return total * (0.5 ** (3 + depth))
+
+        level, coupled_levels = cubes, []
+        for depth in range(6):
+            picked = [dot(child[p], level).astype(BF) for p in range(2)]
+            yield
+            coupled_levels.append(coupled(level, depth))
+            yield
+            level = (dot(picked[0], pair_ref[0]) + dot(picked[1], pair_ref[1])).astype(BF)
+            yield
+        coeffs = coupled(level, 6).astype(BF)
+        yield
+        for depth in range(5, -1, -1):
+            picked = [dot(mother[p], coeffs).astype(BF) for p in range(2)]
+            yield
+            total = coupled_levels[depth]
+            for p in range(2):
+                total = total + dot(picked[p], pair_ref[p], NT)
+            coeffs = total.astype(BF)
+            yield
+        coarse_coeffs.append(coeffs)
+
+    steps = coarse_tree()
     mid_place = mid_list[...].T - (me * 128 - 48)
-    pick(mid_place[0:64], 64, 0, mid_ref[...])
-    pick(mid_place[64:128], 64, 64, mid_ref[...])
+    pick(mid_place[0:64], 64, 0, mid_ref[...], steps)
+    pick(mid_place[64:128], 64, 64, mid_ref[...], steps)
+    for _ in steps:
+        pass
+    coeffs = coarse_coeffs[0]
     pick(top_list[...] - (me * 16 - 16), 16, 128, top_ref[...])
     far = dot(far_pick[0:144, :], weight_ref[...], NT)
-
-    for copy in to_twins:
-        copy.wait()
-    row, col = iota((64, cube_ref.shape[0]), 0), iota((64, cube_ref.shape[0]), 1)
-    cubes = dot(ones_where(col == 16 * (row // 2) + row % 2), cube_ref[...]).astype(BF)
-    row, col = iota((64, 64), 0), iota((64, 64), 1)
-    child = [ones_where(col == 2 * row + p) for p in range(2)]
-    mother = [ones_where((col == row // 2) & (row % 2 == p)) for p in range(2)]
-    shift = [
-        ones_where((col == row - 3) & (row % 2 == 1)),
-        ones_where(col == row - 2),
-        ones_where(col == row + 2),
-        ones_where((col == row + 3) & (row % 2 == 0)),
-    ]
-    levels = [cubes]
-    for _ in range(6):
-        total = None
-        for p in range(2):
-            part = dot(dot(child[p], levels[-1]).astype(BF), pair_ref[p])
-            total = part if total is None else total + part
-        levels.append(total.astype(BF))
-    coeffs = None
-    for depth in range(6, -1, -1):
-        total = None
-        for w in range(4):
-            part = dot(dot(shift[w], levels[depth]).astype(BF), coarse_ref[w], NT)
-            total = part if total is None else total + part
-        total = total * (0.5 ** (3 + depth))
-        if coeffs is not None:
-            for p in range(2):
-                total = total + dot(dot(mother[p], coeffs).astype(BF), pair_ref[p], NT)
-        coeffs = total.astype(BF)
 
     def split_down(coeffs, half, first, start, rows):
         parents = coeffs.shape[0]
@@ -351,7 +370,8 @@
     lax.fori_loop(0, 2, finish_inner, 0)
     lax.fori_loop(2, 4, finish_outer, 0)
 
-    def change_chunk(c, _):
+    def change_chunk(i, _):
+        c = lax.rem(i + 1, 4)
         for copy in to_orbs(near_part, near_other, near_send, near_recv, c, 256):
             copy.wait()
         for copy in to_orbs(coeff_part, coeff_other, coeff_send, coeff_recv, c, 128):

time: 73.8 us -> 69 us (0.935)
  Pallas kernels: 68.1 us -> 63.3 us
    pallas_call x1, Pallas kernels: 68.1 us -> 63.3 us  [shards(): pl.pallas_call(step_kernel, in_specs=[near_by, here, here, here, here, he...]
where the time goes in v7:
time: 69 us; the launch traced here: 68.8 us
  Pallas kernels  63.3 us (92%)
  local copies, waits for them, and re-layouts  3.86 us (6%)
  other arithmetic  1.59 us (2%)
    pallas_call x1, Pallas kernels, shards(): pl.pallas_call(step_kernel, in_specs=[near_by, here, here, here, here, he...  63.3 us
    unnamed x19, local copies, waits for them, and re-layouts  3.86 us
    sub x1, other arithmetic, shards(): return orbitals - RELAX_STEP * change * orbitals  1.59 us

profile of v7, /device:TPU:0, one launch (start us, length us, event | category | flops | bytes accessed | tf_op | source)
XLA Modules:
  0.0 68.8 jit_solution(7181194356474623586)
XLA Ops:
  0.0 0.0 copy-start.3
  0.0 0.0 copy-start.6
  0.0 0.0 copy-start.2
  0.0 0.0 copy-start.5
  0.0 0.0 copy-start.7
  0.0 0.0 copy-start.4
  0.0 0.0 copy-start
  0.0 0.0 copy-start.1
  0.0 3.8 %copy.12.coupling_hbm = bf16[108,64,64]{2,1,0:T(8,128)(2,1)S(1)} copy(bf16[108,64,64]{0,2,1:T(8,128)(2,1)} %param.19) | data formatting | bytes 1769472 | tf_op args[8]
  3.9 0.0 copy-done.3
  3.9 0.0 copy-done.6
  3.9 0.0 copy-done.2
  3.9 0.0 copy-done.5
  3.9 0.0 copy-done.7
  3.9 0.0 copy-done.4
  3.9 0.0 copy-done
  3.9 0.0 copy-done.1
  4.0 0.0 copy-start.8
  4.0 63.3 %step.1 = f32[2,1024,256]{2,1,0:T(8,128)S(1)} custom-call(f32[2,1024,256]{2,1,0:T(8,128)} %orb_hbm.1, s32[27,1024]{1,0:T(8,128)S(1)} %bitcast.4, s32[108,1024]{1,0:T(8,128)S(1)} %bitcast.3, s32[108,128]{1,0:T(8,128)S(1)} %bitcast.5, s32[16,108]{1,0:T(8,128)S(1)} %copy-done.7, bf16[64,256]{1,0:T(8,128)(2,1)S(1)} %copy-done.5, ...), custom_call_target="tpu_custom_call" | custom-call | flops 35999997952 | bytes 12582912 | tf_op jit(solution)/shard_map/step/pallas_call | solution.py:401
  67.2 0.0 copy-done.8
  67.2 1.6 %multiply_subtract_fusion = f32[2,1024,256]{2,1,0:T(8,128)} fusion(f32[2,1024,256]{2,1,0:T(8,128)S(1)} %copy-done.8, f32[2,1024,256]{2,1,0:T(8,128)S(1)} %step.1), kind=kLoop, calls=%fused_computation | loop fusion | flops 1572864 | bytes 6291456 | tf_op jit(solution)/shard_map/sub | solution.py:446
Async XLA Ops:
  0.0 3.9 %copy-start.3 = (bf16[4,64,64]{2,1,0:T(8,128)(2,1)S(1)}, bf16[4,64,64]{2,1,0:T(8,128)(2,1)}, u32[]{:S(2)}) copy-start(bf16[4,64,64]{2,1,0:T(8,128)(2,1)} %coarse_in.1) | copy-start | bytes 98308
  0.0 3.9 %copy-start.6 = (bf16[2,64,64]{2,1,0:T(8,128)(2,1)S(1)}, bf16[2,64,64]{2,1,0:T(8,128)(2,1)}, u32[]{:S(2)}) copy-start(bf16[2,64,64]{2,1,0:T(8,128)(2,1)} %pair_in.1) | copy-start | bytes 49156
  0.0 3.9 %copy-start.2 = (bf16[8,64,64]{2,1,0:T(8,128)(2,1)S(1)}, bf16[8,64,64]{2,1,0:T(8,128)(2,1)}, u32[]{:S(2)}) copy-start(bf16[8,64,64]{2,1,0:T(8,128)(2,1)} %transfer_in.1) | copy-start | bytes 196612
  0.0 3.9 %copy-start.5 = (bf16[64,256]{1,0:T(8,128)(2,1)S(1)}, bf16[64,256]{1,0:T(8,128)(2,1)}, u32[]{:S(2)}) copy-start(bf16[64,256]{1,0:T(8,128)(2,1)} %basis_ref.1) | copy-start | bytes 98308
  0.0 3.9 %copy-start.7 = (s32[16,108]{1,0:T(8,128)S(1)}, s32[16,108]{1,0:T(8,128)}, u32[]{:S(2)}) copy-start(s32[16,108]{1,0:T(8,128)} %top_list.1) | copy-start | bytes 20740
  0.0 3.9 %copy-start.4 = (s32[128,108]{0,1:T(8,128)S(1)}, s32[128,108]{0,1:T(8,128)}, u32[]{:S(2)}) copy-start(s32[128,108]{0,1:T(8,128)} %param.14) | copy-start | bytes 165892
  0.0 3.9 %copy-start = (s32[1024,108]{0,1:T(8,128)S(1)}, s32[1024,108]{0,1:T(8,128)}, u32[]{:S(2)}) copy-start(s32[1024,108]{0,1:T(8,128)} %param.13) | copy-start | bytes 1327108
  0.0 3.9 %copy-start.1 = (s32[1024,27]{0,1:T(8,128)S(1)}, s32[1024,27]{0,1:T(8,128)}, u32[]{:S(2)}) copy-start(s32[1024,27]{0,1:T(8,128)} %param.12) | copy-start | bytes 331780
  4.0 63.3 %copy-start.8 = (f32[2,1024,256]{2,1,0:T(8,128)S(1)}, f32[2,1024,256]{2,1,0:T(8,128)}, u32[]{:S(2)}) copy-start(f32[2,1024,256]{2,1,0:T(8,128)} %orb_hbm.1) | copy-start | bytes 6291460

commit v8 on v7

--- a/solution.py
+++ b/solution.py
@@ -37,11 +37,15 @@
     return numbers.astype(F32).astype(BF)
 
 
+def log2(number):
+    return number.bit_length() - 1
+
+
 def octant_picker(parents, half, width):
     row, col = iota((8 * parents, width), 0), iota((8 * parents, width), 1)
-    octant, b = row // parents, row % parents
-    z, y, x = b // (half * half), (b // half) % half, b % half
-    dz, dy, dx = octant // 4, (octant // 2) % 2, octant % 2
+    octant, b = row >> log2(parents), row & (parents - 1)
+    z, y, x = b >> (2 * log2(half)), (b >> log2(half)) & (half - 1), b & (half - 1)
+    dz, dy, dx = octant >> 2, (octant >> 1) & 1, octant & 1
     side = 2 * half
     child = ((2 * z + dz) * side + 2 * y + dy) * side + 2 * x + dx
     return ones_where(child == col)
@@ -70,7 +74,7 @@
 def step_kernel(
     orb_hbm, near_list, leaf_list, mid_list, top_list, basis_ref, table_hbm, transfer_in, coupling_hbm, pair_in, coarse_in,
     out_ref,
-    orb_ref, table_ref, coupling_ref, dens_ref, leaf_ref, mid_ref, top_ref, cube_ref, basis2_ref, transfer_ref, pair_ref,
+    orb_ref, table_ref, coupling_ref, picker_ref, dens_ref, leaf_ref, mid_ref, top_ref, cube_ref, basis2_ref, transfer_ref, pair_ref,
     coarse_ref, weight_ref, near_pick, far_pick, near_ref, near_part, near_other, far_ref, coeff_ref, coeff_part, coeff_other,
     load_sem, halo_send, halo_recv, cube_send, cube_recv, near_send, near_recv, coeff_send, coeff_recv,
 ):
@@ -85,8 +89,6 @@
     twins = [lax.rem(me + away, count) for away in range(group, count, group)]
     friends = [(other, orb) for other in mates + twins + [before, after]]
     friends += [(me, lax.rem(orb + away, orbs)) for away in range(1, orbs)]
-    for friend in friends:
-        pl.semaphore_signal(barrier, inc=1, device_id=friend, device_id_type=MESH)
 
     def rows_of(c, size):
         return pl.ds(pl.multiple_of(c * size, size), size)
@@ -101,11 +103,14 @@
         load_orbitals(c).start()
     load_table.start()
     load_coupling.start()
+    for friend in friends:
+        pl.semaphore_signal(barrier, inc=1, device_id=friend, device_id_type=MESH)
 
     spread_basis(basis_ref, basis2_ref)
     for given, kept in ((pair_in, pair_ref), (coarse_in, coarse_ref), (transfer_in, transfer_ref)):
         for i in range(given.shape[0]):
             kept[i] = spread(given[i])
+    picker_ref[...] = octant_picker(32, 4, 256)
     mid_ref[224:256, :] = jnp.zeros((32, 128), BF)
     top_ref[48:128, :] = jnp.zeros((80, 128), BF)
 
@@ -118,7 +123,7 @@
             dens_ref[inner, o * 256 : (o + 1) * 256] = (values * values).astype(BF)
         leaf = dot(dens_ref[inner, :], basis2_ref[...], NT).astype(BF)
         leaf_ref[pl.ds(pl.multiple_of(192 + c * 256, 64), 256), :] = leaf
-        picked = dot(octant_picker(32, 4, 256), leaf).astype(BF)
+        picked = dot(picker_ref[...], leaf).astype(BF)
         mid_ref[pl.ds(pl.multiple_of(48 + c * 32, 16), 32), :] = merge_up(picked, 32, transfer_ref)
         return 0
 
@@ -331,11 +336,11 @@
         parents = coeffs.shape[0]
         side = 2 * half
         row, col = iota((rows, parents), 0) + start, iota((rows, parents), 1)
-        z, y, x = row // (side * side), (row // side) % side, row % side
-        parent = ((z // 2) * half + y // 2) * half + x // 2 + first
+        z, y, x = row >> (2 * log2(side)), (row >> log2(side)) & (side - 1), row & (side - 1)
+        parent = ((z >> 1) * half + (y >> 1)) * half + (x >> 1) + first
         pulled = dot(ones_where(col == parent), coeffs).astype(BF)
         r = iota((rows, 128), 0) + start
-        octant = 4 * ((r // (side * side)) % 2) + 2 * ((r // side) % 2) + r % 2
+        octant = 4 * ((r >> (2 * log2(side))) & 1) + 2 * ((r >> log2(side)) & 1) + (r & 1)
         total = None
         for o in range(8):
             part = dot(jnp.where(octant == o, pulled, jnp.zeros_like(pulled)), transfer_ref[o], NT)
@@ -407,6 +412,7 @@
             pltpu.VMEM((2, 1024, 256), F32),
             pltpu.VMEM((27, 256, 256), BF),
             pltpu.VMEM((108, 64, 64), BF),
+            pltpu.VMEM((256, 256), BF),
             pltpu.VMEM((1152, 512), BF),
             pltpu.VMEM((1408, 128), BF),
             pltpu.VMEM((256, 128), BF),

time: 69 us -> 67 us (0.971)
  Pallas kernels: 63.3 us -> 61.3 us
    pallas_call x1, Pallas kernels: 63.3 us -> 61.3 us  [shards(): pl.pallas_call(step_kernel, in_specs=[near_by, here, here, here, here, he...]
where the time goes in v8:
time: 67 us; the launch traced here: 66.8 us
  Pallas kernels  61.3 us (91%)
  local copies, waits for them, and re-layouts  3.86 us (6%)
  other arithmetic  1.59 us (2%)
    pallas_call x1, Pallas kernels, shards(): pl.pallas_call(step_kernel, in_specs=[near_by, here, here, here, here, he...  61.3 us
    unnamed x19, local copies, waits for them, and re-layouts  3.86 us
    sub x1, other arithmetic, shards(): return orbitals - RELAX_STEP * change * orbitals  1.59 us

profile of v8, /device:TPU:0, one launch (start us, length us, event | category | flops | bytes accessed | tf_op | source)
XLA Modules:
  0.0 66.8 jit_solution(7215424570881848065)
XLA Ops:
  0.0 0.0 copy-start.3
  0.0 0.0 copy-start.6
  0.0 0.0 copy-start.2
  0.0 0.0 copy-start.5
  0.0 0.0 copy-start.7
  0.0 0.0 copy-start.4
  0.0 0.0 copy-start
  0.0 0.0 copy-start.1
  0.0 3.8 %copy.12.coupling_hbm = bf16[108,64,64]{2,1,0:T(8,128)(2,1)S(1)} copy(bf16[108,64,64]{0,2,1:T(8,128)(2,1)} %param.19) | data formatting | bytes 1769472 | tf_op args[8]
  3.9 0.0 copy-done.3
  3.9 0.0 copy-done.6
  3.9 0.0 copy-done.2
  3.9 0.0 copy-done.5
  3.9 0.0 copy-done.7
  3.9 0.0 copy-done.4
  3.9 0.0 copy-done
  3.9 0.0 copy-done.1
  4.0 0.0 copy-start.8
  4.0 61.3 %step.1 = f32[2,1024,256]{2,1,0:T(8,128)S(1)} custom-call(f32[2,1024,256]{2,1,0:T(8,128)} %orb_hbm.1, s32[27,1024]{1,0:T(8,128)S(1)} %bitcast.4, s32[108,1024]{1,0:T(8,128)S(1)} %bitcast.3, s32[108,128]{1,0:T(8,128)S(1)} %bitcast.5, s32[16,108]{1,0:T(8,128)S(1)} %copy-done.7, bf16[64,256]{1,0:T(8,128)(2,1)S(1)} %copy-done.5, ...), custom_call_target="tpu_custom_call" | custom-call | flops 35999997952 | bytes 12582912 | tf_op jit(solution)/shard_map/step/pallas_call | solution.py:406
  65.2 0.0 copy-done.8
  65.3 1.6 %multiply_subtract_fusion = f32[2,1024,256]{2,1,0:T(8,128)} fusion(f32[2,1024,256]{2,1,0:T(8,128)S(1)} %copy-done.8, f32[2,1024,256]{2,1,0:T(8,128)S(1)} %step.1), kind=kLoop, calls=%fused_computation | loop fusion | flops 1572864 | bytes 6291456 | tf_op jit(solution)/shard_map/sub | solution.py:452
Async XLA Ops:
  0.0 3.9 %copy-start.3 = (bf16[4,64,64]{2,1,0:T(8,128)(2,1)S(1)}, bf16[4,64,64]{2,1,0:T(8,128)(2,1)}, u32[]{:S(2)}) copy-start(bf16[4,64,64]{2,1,0:T(8,128)(2,1)} %coarse_in.1) | copy-start | bytes 98308
  0.0 3.9 %copy-start.6 = (bf16[2,64,64]{2,1,0:T(8,128)(2,1)S(1)}, bf16[2,64,64]{2,1,0:T(8,128)(2,1)}, u32[]{:S(2)}) copy-start(bf16[2,64,64]{2,1,0:T(8,128)(2,1)} %pair_in.1) | copy-start | bytes 49156
  0.0 3.9 %copy-start.2 = (bf16[8,64,64]{2,1,0:T(8,128)(2,1)S(1)}, bf16[8,64,64]{2,1,0:T(8,128)(2,1)}, u32[]{:S(2)}) copy-start(bf16[8,64,64]{2,1,0:T(8,128)(2,1)} %transfer_in.1) | copy-start | bytes 196612
  0.0 3.9 %copy-start.5 = (bf16[64,256]{1,0:T(8,128)(2,1)S(1)}, bf16[64,256]{1,0:T(8,128)(2,1)}, u32[]{:S(2)}) copy-start(bf16[64,256]{1,0:T(8,128)(2,1)} %basis_ref.1) | copy-start | bytes 98308
  0.0 3.9 %copy-start.7 = (s32[16,108]{1,0:T(8,128)S(1)}, s32[16,108]{1,0:T(8,128)}, u32[]{:S(2)}) copy-start(s32[16,108]{1,0:T(8,128)} %top_list.1) | copy-start | bytes 20740
  0.0 3.9 %copy-start.4 = (s32[128,108]{0,1:T(8,128)S(1)}, s32[128,108]{0,1:T(8,128)}, u32[]{:S(2)}) copy-start(s32[128,108]{0,1:T(8,128)} %param.14) | copy-start | bytes 165892
  0.0 3.9 %copy-start = (s32[1024,108]{0,1:T(8,128)S(1)}, s32[1024,108]{0,1:T(8,128)}, u32[]{:S(2)}) copy-start(s32[1024,108]{0,1:T(8,128)} %param.13) | copy-start | bytes 1327108
  0.0 3.9 %copy-start.1 = (s32[1024,27]{0,1:T(8,128)S(1)}, s32[1024,27]{0,1:T(8,128)}, u32[]{:S(2)}) copy-start(s32[1024,27]{0,1:T(8,128)} %param.12) | copy-start | bytes 331780
  4.0 61.3 %copy-start.8 = (f32[2,1024,256]{2,1,0:T(8,128)S(1)}, f32[2,1024,256]{2,1,0:T(8,128)}, u32[]{:S(2)}) copy-start(f32[2,1024,256]{2,1,0:T(8,128)} %orb_hbm.1) | copy-start | bytes 6291460
